TPU v7x, 128 devices: a whole 4x4x4 slice. The times are simulated.
128 devices in a mesh: stream: 32 (over y_hi, z, x), depth: 4 (over y_lo, core).
Axes of the slice: x: 4, y: 4 (y_hi: 2, y_lo: 2; y = y_hi * 2 + y_lo), z: 4, core: 2. Of those that a mesh axis runs over, the one named last changes fastest.
Arguments:
- populations: float32 [27, 128, 64, 128], P(None, 'stream', 'depth'), may hold values from 0 to 1, as said below
- moment_rates: float32 [27], replicated, may hold values from 0.6 to 1.9
- solid_bricks: int32 [32, 16, 32], P('stream', 'depth'), may hold values 0 or 1
- owners: int32 [16384, 1], P(('stream', 'depth')), may hold values from 0 to 127; in each aligned block of 128 rows (0 to 127, 128 to 255, ...) at most 2 rows name the same one
- bricks: int32 [16384], P(('stream', 'depth')), may hold values from 0 to 127
- levels: int32 [16384], P(('stream', 'depth')), may hold values from 1 to 2
Outputs:
- advanced: float32 [27, 128, 64, 128], P(None, 'stream', 'depth')
- ghosts: float32 [16384, 2, 1728], P(('stream', 'depth'))
Inputs may be any that keep to these rules, and one draw needn't show every extreme that they name: `owners`: among the 128 entries of one device at most 2 name the same owner, and some device names some owner exactly 2 times. `populations`: populations are positive.
All inputs are finite; a program needn't handle non-finite values. No bound on the sum of `solid_bricks` on one device may be relied on, other than what follows from the above.
Results may differ from a plain program's by a relative error of at most 0.0001.
Values sent between devices are 32-bit elements; how exact they have to be, the bound alone decides.
A program may use at most 128 MiB of HBM per device.

v0:
```python
import jax
import jax.numpy as jnp
import numpy as np
from jax import lax
from jax.sharding import PartitionSpec as P

BRICK = 4
CAP = 2


power_table = np.array([[1.0, 1.0, 1.0], [-1.0, 0.0, 1.0], [1.0, 0.0, 1.0]])
inverse_table = np.array([[0.0, -0.5, 0.5], [1.0, 0.0, -1.0], [0.0, 0.5, 0.5]])
line_weights = np.array([1.0 / 6.0, 2.0 / 3.0, 1.0 / 6.0])
lattice_x = np.repeat(np.array([-1.0, 0.0, 1.0]), 9)
lattice_y = np.tile(np.repeat(np.array([-1.0, 0.0, 1.0]), 3), 3)
lattice_z = np.tile(np.array([-1.0, 0.0, 1.0]), 9)
lattice_weights = np.kron(np.kron(line_weights, line_weights), line_weights)


def extended(value, sides, width):
    for axis, dim in sides:
        size, length = (lax.axis_size(axis), value.shape[dim])
        up = [(i, (i + 1) % size) for i in range(size)]
        down = [(j, i) for i, j in up]
        last = lax.slice_in_dim(value, length - width, length, axis=dim)
        initial = lax.slice_in_dim(value, 0, width, axis=dim)
        before = lax.ppermute(last, axis, up)
        after = lax.ppermute(initial, axis, down)
        value = jnp.concatenate([before, value, after], axis=dim)
    return value


def equilibrium(popul):
    extra = popul.ndim - 1
    grouped = popul.reshape((3, 3, 3) + popul.shape[1:])
    density = jnp.sum(popul, axis=0)
    moment_x = jnp.sum(grouped[2], axis=(0, 1)) - jnp.sum(grouped[0], axis=(0, 1))
    moment_y = jnp.sum(grouped[:, 2], axis=(0, 1)) - jnp.sum(grouped[:, 0], axis=(0, 1))
    moment_z = jnp.sum(grouped[:, :, 2], axis=(0, 1)) - jnp.sum(grouped[:, :, 0], axis=(0, 1))
    speed_x = moment_x / density
    speed_y = moment_y / density
    speed_z = moment_z / density
    shape_col = (27,) + (1,) * extra
    along_x = jnp.asarray(lattice_x, jnp.float32).reshape(shape_col)
    along_y = jnp.asarray(lattice_y, jnp.float32).reshape(shape_col)
    along_z = jnp.asarray(lattice_z, jnp.float32).reshape(shape_col)
    weights = jnp.asarray(lattice_weights, jnp.float32).reshape(shape_col)
    projected = along_x * speed_x + along_y * speed_y + along_z * speed_z
    squared = speed_x * speed_x + speed_y * speed_y + speed_z * speed_z
    return weights * density * (1.0 + 3.0 * projected + 4.5 * projected * projected - 1.5 * squared)


def relax_matrix(moment_rates):
    moment = jnp.asarray(np.kron(np.kron(power_table, power_table), power_table), jnp.float32)
    inverse = jnp.asarray(
        np.kron(np.kron(inverse_table, inverse_table), inverse_table), jnp.float32
    )
    return jnp.dot(inverse * moment_rates[None, :], moment, precision=lax.Precision.HIGHEST)


def collide(flattened, solid_cells, relaxer):
    balance = equilibrium(flattened)
    relaxed = flattened - jnp.dot(relaxer, flattened - balance, precision=lax.Precision.HIGHEST)
    return jnp.where(solid_cells[None, :], flattened[::-1], relaxed)


def roll_span(grouped_z):
    return jnp.stack(
        [jnp.roll(grouped_z[0], -1, axis=-1), grouped_z[1], jnp.roll(grouped_z[2], 1, axis=-1)]
    )


def stream_padded(padded, width_x, width_y):
    grouped = padded.reshape((3, 3, 3) + padded.shape[1:])
    pieces = []
    for along_x in range(3):
        for along_y in range(3):
            window = grouped[
                along_x,
                along_y,
                :,
                2 - along_x : 2 - along_x + width_x,
                2 - along_y : 2 - along_y + width_y,
            ]
            pieces.append(roll_span(window))
    return jnp.stack(pieces).reshape((27, width_x, width_y, padded.shape[-1]))


def rescale(chosen, levels, moment_rates):
    entries = chosen.shape[0]
    grouped = chosen.reshape(entries, 27, BRICK**3).transpose(1, 0, 2)
    balance = equilibrium(grouped)
    tau_coarse = 1.0 / moment_rates[12]
    spacing = jnp.where(levels == 2, 4.0, 2.0).astype(jnp.float32)
    tau_fine = 0.5 + spacing * (tau_coarse - 0.5)
    factor = (tau_fine / (spacing * tau_coarse))[None, :, None]
    fine_blocks = balance + factor * (grouped - balance)
    return fine_blocks.transpose(1, 0, 2).reshape(entries, 27 * BRICK**3)


def per_device(populations, moment_rates, solid_bricks, owners, bricks, levels):
    width_x, width_y, width_z = (populations.shape[1], populations.shape[2], populations.shape[3])
    cells_all = width_x * width_y * width_z
    bricks_x, bricks_y, bricks_z = solid_bricks.shape
    relaxer = relax_matrix(moment_rates)
    expanded = jnp.broadcast_to(
        solid_bricks[:, None, :, None, :, None], (bricks_x, BRICK, bricks_y, BRICK, bricks_z, BRICK)
    )
    solid_cells = expanded.reshape(cells_all) > 0
    current = populations
    for substep in range(2):
        collided = collide(current.reshape(27, cells_all), solid_cells, relaxer).reshape(
            populations.shape
        )
        padded = extended(collided, (("stream", 1), ("depth", 2)), 1)
        current = stream_padded(padded, width_x, width_y)
    block_size = 27 * BRICK**3
    brick_table = current.reshape(27, bricks_x, BRICK, bricks_y, BRICK, bricks_z, BRICK)
    brick_table = brick_table.transpose(1, 3, 5, 0, 2, 4, 6).reshape(
        bricks_x * bricks_y * bricks_z, block_size
    )
    chosen = jnp.take(brick_table, bricks, axis=0)
    fine_blocks = rescale(chosen, levels, moment_rates)
    list_len = bricks.shape[0]
    owner_col = owners[:, 0]
    same_owner = owner_col[:, None] == owner_col[None, :]
    earlier = (
        jnp.arange(list_len, dtype=jnp.int32)[None, :]
        < jnp.arange(list_len, dtype=jnp.int32)[:, None]
    )
    slot_rank = jnp.sum((same_owner & earlier).astype(jnp.int32), axis=1)
    slot_index = owner_col * CAP + slot_rank
    stream_count = lax.axis_size("stream")
    depth_count = lax.axis_size("depth")
    device_count = stream_count * depth_count
    slot_numbers = jnp.arange(device_count * CAP, dtype=jnp.int32)
    placement_matrix = (slot_numbers[:, None] == slot_index[None, :]).astype(jnp.float32)
    outgoing = jnp.dot(placement_matrix, fine_blocks, precision=lax.Precision.HIGHEST)
    ghosts = lax.all_to_all(
        outgoing.reshape(device_count, CAP, block_size),
        ("stream", "depth"),
        split_axis=0,
        concat_axis=0,
        tiled=True,
    )
    return (current, ghosts)


def solution(mesh):
    return jax.shard_map(
        per_device,
        mesh=mesh,
        in_specs=(
            P(None, "stream", "depth", None),
            P(),
            P("stream", "depth", None),
            P(("stream", "depth"), None),
            P(("stream", "depth")),
            P(("stream", "depth")),
        ),
        out_specs=(P(None, "stream", "depth", None), P(("stream", "depth"), None, None)),
        check_vma=False,
    )
```

profile of v0, /device:TPU:1, one launch (start us, length us, event | category | flops | bytes accessed | tf_op | source)
XLA Modules:
  0.0 171.7 jit_solution(1355211476066284897)
XLA Ops:
  0.6 1.6 reshape_reshape.9
  2.2 0.2 slice_reduce_fusion.2
  2.4 0.5 slice_reduce_fusion.12
  3.2 0.6 copy.60
  3.9 1.7 rev.6
  5.8 0.8 gt.20
  6.8 1.6 fusion.1
  8.5 0.2 copy.61
  8.8 2.1 %collective-permute-start = (f32[27,1,16,128]{3,2,1,0:T(8,128)S(1)}, f32[27,1,16,128]{3,2,1,0:T(8,128)S(1)}, u32[]{:S(2)}, u32[]{:S(2)}) collective-permute-start(f32[27,1,16,128]{3,2,1,0:T(8,128)S(1)} %get-tuple-element.109), channel_id=1, source_target_pairs={{0,4},{4,8},{8,12},{12,16},{16,20},{20,24},{24,28},{28,32},{32,36}... | collective-permute-start | bytes 663560 | tf_op jit(solution)/shard_map/ppermute | solution.py:27
  10.9 7.5 %collective-permute-start.1 = (f32[27,1,16,128]{3,2,1,0:T(8,128)S(1)}, f32[27,1,16,128]{3,2,1,0:T(8,128)S(1)}, u32[]{:S(2)}, u32[]{:S(2)}) collective-permute-start(f32[27,1,16,128]{3,2,1,0:T(8,128)S(1)} %get-tuple-element.108), channel_id=1, source_target_pairs={{4,0},{8,4},{12,8},{16,12},{20,16},{24,20},{28,24},{32,28},{36,32}... | collective-permute-start | bytes 663560 | tf_op jit(solution)/shard_map/ppermute | solution.py:28
  18.3 0.6 slice.797
  19.3 0.7 mul.421
  20.0 0.7 mul.427
  20.9 0.6 multiply_add_fusion.1
  22.2 0.6 compare_and_fusion
  22.8 0.7 collective-permute-done
  23.7 1.6 collective-permute-start.2
  25.3 0.6 pad_clamp_fusion
  25.8 0.9 collective-permute-done.2
  26.7 2.4 %collective-permute-done.3 = f32[27,6,1,128]{3,2,1,0:T(1,128)S(1)} collective-permute-done((f32[27,6,1,128]{3,2,1,0:T(1,128)S(1)}, f32[27,6,1,128]{3,2,1,0:T(1,128)S(1)}, u32[]{:S(2)}, u32[]{:S(2)}) %collective-permute-start.3) | collective-permute-done | bytes 82976 | tf_op jit(solution)/shard_map/ppermute | solution.py:28
  29.1 0.3 pad_maximum_fusion
  30.6 0.7 pad_maximum_fusion.14
  31.5 0.7 pad_maximum_fusion.15
  32.3 0.7 pad_maximum_fusion.12
  33.1 0.7 pad_maximum_fusion.13
  34.0 0.7 pad_maximum_fusion.10
  34.8 0.7 pad_maximum_fusion.11
  35.7 0.7 pad_maximum_fusion.8
  36.5 0.7 pad_maximum_fusion.9
  37.4 0.7 pad_maximum_fusion.6
  38.2 0.7 pad_maximum_fusion.7
  39.0 0.7 pad_maximum_fusion.4
  39.9 0.7 pad_maximum_fusion.5
  40.7 0.7 pad_maximum_fusion.2
  41.6 0.7 pad_maximum_fusion.3
  42.5 0.4 reshape_reshape_reshape.3
  42.9 1.1 slice_reduce_fusion.10
  44.0 0.8 slice_reduce_fusion
  45.2 1.7 rev.7
  47.2 1.6 fusion
  49.2 0.3 collective-permute-start.4
  49.5 0.2 copy-done.42
  49.7 0.6 multiply_divide_fusion
  50.3 7.8 %collective-permute-start.5 = (f32[27,1,16,128]{3,2,1,0:T(8,128)S(1)}, f32[27,1,16,128]{3,2,1,0:T(8,128)S(1)}, u32[]{:S(2)}, u32[]{:S(2)}) collective-permute-start(f32[27,1,16,128]{3,2,1,0:T(8,128)S(1)} %get-tuple-element.106), channel_id=1, source_target_pairs={{4,0},{8,4},{12,8},{16,12},{20,16},{24,20},{28,24},{32,28},{36,32}... | collective-permute-start | bytes 663560 | tf_op jit(solution)/shard_map/ppermute | solution.py:28
  58.1 4.4 %collective-permute-done.4 = f32[27,1,16,128]{3,2,1,0:T(8,128)S(1)} collective-permute-done((f32[27,1,16,128]{3,2,1,0:T(8,128)S(1)}, f32[27,1,16,128]{3,2,1,0:T(8,128)S(1)}, u32[]{:S(2)}, u32[]{:S(2)}) %collective-permute-start.4) | collective-permute-done | bytes 221216 | tf_op jit(solution)/shard_map/ppermute | solution.py:27
  62.6 0.4 collective-permute-done.5
  63.1 0.6 collective-permute-start.6
  63.7 0.5 multiply_add_fusion
  64.3 0.9 collective-permute-done.6
  65.2 2.4 %collective-permute-done.7 = f32[27,6,1,128]{3,2,1,0:T(1,128)S(1)} collective-permute-done((f32[27,6,1,128]{3,2,1,0:T(1,128)S(1)}, f32[27,6,1,128]{3,2,1,0:T(1,128)S(1)}, u32[]{:S(2)}, u32[]{:S(2)}) %collective-permute-start.7) | collective-permute-done | bytes 82976 | tf_op jit(solution)/shard_map/ppermute | solution.py:28
  67.6 0.3 pad_maximum_fusion.1
  70.4 30.6 %reshape_reshape.11 = f32[27,1,4,4,4,32,4]{6,5,4,3,2,0,1:T(8,128)} reshape(f32[9,3,4,16,128]{4,3,2,1,0:T(8,128)S(1)} %fusion.86) | data formatting | bytes 1769472 | tf_op jit(solution)/shard_map/reshape;reshape | solution.py:118
  101.0 17.3 %copy.54 = f32[1,4,32,27,4,4,4]{2,1,6,5,4,3,0:T(4,128)S(1)} copy(f32[1,4,32,27,4,4,4]{6,2,5,1,4,3,0:T(8,128)} %bitcast.405) | data formatting | bytes 1769472 | tf_op jit(solution)/shard_map/transpose | solution.py:119
  118.3 2.3 %reshape.1016 = f32[128,1728]{0,1:T(8,128)} reshape(f32[1,4,32,27,4,4,4]{2,1,6,5,4,3,0:T(4,128)S(1)} %copy.54) | data formatting | bytes 1769472 | tf_op jit(solution)/shard_map/reshape | solution.py:119
  120.7 1.5 copy.55
  122.1 1.1 gather_fusion
  123.2 0.3 copy.56
  123.5 0.4 copy-done.30
  124.2 0.5 copy-done.20
  124.7 1.0 fusion.30
  125.7 2.1 %fusion.31 = f32[128,2,1728]{0,2,1:T(8,128)} fusion(f32[128,1728]{0,1:T(8,128)S(1)} %fusion.30, f32[128,1728]{0,1:T(8,128)S(1)} %copy.56, f32[128]{0:T(128)S(1)} %copy-done.28, pred[128]{0:T(512)(128)(4,1)S(1)} %copy-done.30, s32[128]{0:T(128)S(1)} %copy-done.33, s32[128,2]{0,1:T(2,128)S(1)} %copy-done.31), kind=kOutput, calls=%fused_computation.37 | convolution fusion | flops 680394752 | bytes 3541120 | tf_op jit(solution)/shard_map/dot_general | solution.py:138
  127.9 2.9 %copy.58 = f32[128,2,1728]{2,1,0:T(2,128)S(1)} copy(f32[128,2,1728]{0,2,1:T(8,128)} %fusion.31) | data formatting | bytes 3538944 | tf_op jit(solution)/shard_map/dot_general | solution.py:138
  130.8 37.0 %all_to_all.5 = f32[128,2,1728]{2,1,0:T(2,128)} all-to-all(f32[128,2,1728]{2,1,0:T(2,128)S(1)} %copy.58), channel_id=1, replica_groups=mesh['stream'=32,'depth'=4] {'stream','depth'}, dimensions={0} | all-to-all | bytes 3538944 | tf_op jit(solution)/shard_map/all_to_all | solution.py:139
  167.8 3.9 %copy.59 = f32[128,2,1728]{0,2,1:T(8,128)} copy(f32[128,2,1728]{2,1,0:T(2,128)} %all_to_all.5) | data formatting | bytes 3538944
  (215 shorter events, 8.2 us)
Async XLA Ops:
  0.6 2.3 %copy-start = (f32[27,4,16,128]{3,2,1,0:T(8,128)S(1)}, f32[27,4,16,128]{3,2,1,0:T(8,128)}, u32[]{:S(2)}) copy-start(f32[27,4,16,128]{3,2,1,0:T(8,128)} %param.20) | copy-start | bytes 2654212
  3.8 1.8 %copy-start.29 = (s32[1,4,32]{2,1,0:T(4,128)S(1)}, s32[1,4,32]{2,1,0:T(4,128)}, u32[]{:S(2)}) copy-start(s32[1,4,32]{2,1,0:T(4,128)} %param.22) | copy-start | bytes 1540
  3.8 2.7 %copy-start.24 = (f32[27,27]{1,0:T(8,128)S(1)}, f32[27,27]{1,0:T(8,128)}, u32[]{:S(2)}) copy-start(f32[27,27]{1,0:T(8,128)} %constant.59.clone) | copy-start | bytes 8752
  3.8 2.7 %copy-start.25 = (f32[27,27]{1,0:T(8,128)S(1)}, f32[27,27]{1,0:T(8,128)}, u32[]{:S(2)}) copy-start(f32[27,27]{1,0:T(8,128)} %constant.60.clone) | copy-start | bytes 8752
  3.8 2.7 %copy-start.32 = (f32[27]{0:T(128)S(1)}, f32[27]{0:T(128)}, u32[]{:S(2)}) copy-start(f32[27]{0:T(128)} %param.21) | copy-start | bytes 328
  3.8 2.9 %copy-start.34 = (f32[27]{0:T(128)S(1)}, f32[27]{0:T(128)}, u32[]{:S(2)}) copy-start(f32[27]{0:T(128)} %constant.61.clone) | copy-start | bytes 328
  3.9 2.9 %copy-start.36 = (f32[27]{0:T(128)S(1)}, f32[27]{0:T(128)}, u32[]{:S(2)}) copy-start(f32[27]{0:T(128)} %constant.62.clone) | copy-start | bytes 328
  3.9 2.9 %copy-start.38 = (f32[27]{0:T(128)S(1)}, f32[27]{0:T(128)}, u32[]{:S(2)}) copy-start(f32[27]{0:T(128)} %constant.63.clone) | copy-start | bytes 328
  3.9 2.9 %copy-start.40 = (f32[27]{0:T(128)S(1)}, f32[27]{0:T(128)}, u32[]{:S(2)}) copy-start(f32[27]{0:T(128)} %constant.64.clone) | copy-start | bytes 328
  6.5 1.9 %copy-start.26 = (pred[8192]{0:T(1024)(128)(4,1)}, pred[8192]{0:T(1024)(128)(4,1)S(1)}, u32[]{:S(2)}) copy-start(pred[8192]{0:T(1024)(128)(4,1)S(1)} %gt.20) | copy-start | bytes 24580
  6.7 1.7 %copy-start.22 = (f32[27,27]{1,0:T(8,128)}, f32[27,27]{1,0:T(8,128)S(1)}, u32[]{:S(2)}) copy-start(f32[27,27]{1,0:T(8,128)S(1)} %fusion.90) | copy-start | bytes 8752
  8.7 10.3 %copy-start.44 = (s32[128]{0:T(128)S(1)}, s32[128]{0:T(128)}, u32[]{:S(2)}) copy-start(s32[128]{0:T(128)} %param.24) | copy-start | bytes 1540
  8.7 12.0 %copy-start.43 = (s32[128,1]{0,1:T(1,128)S(1)}, s32[128,1]{0,1:T(1,128)}, u32[]{:S(2)}) copy-start(s32[128,1]{0,1:T(1,128)} %param.23) | copy-start | bytes 1540
  8.8 14.6 %collective-permute-start = (f32[27,1,16,128]{3,2,1,0:T(8,128)S(1)}, f32[27,1,16,128]{3,2,1,0:T(8,128)S(1)}, u32[]{:S(2)}, u32[]{:S(2)}) collective-permute-start(f32[27,1,16,128]{3,2,1,0:T(8,128)S(1)} %get-tuple-element.109), channel_id=1, source_target_pairs={{0,4},{4,8},{8,12},{12,16},{16,20},{20,24},{24,28},{28,32},{32,36}... | collective-permute-start | bytes 663560 | tf_op jit(solution)/shard_map/ppermute | solution.py:27
  10.9 12.6 %collective-permute-start.1 = (f32[27,1,16,128]{3,2,1,0:T(8,128)S(1)}, f32[27,1,16,128]{3,2,1,0:T(8,128)S(1)}, u32[]{:S(2)}, u32[]{:S(2)}) collective-permute-start(f32[27,1,16,128]{3,2,1,0:T(8,128)S(1)} %get-tuple-element.108), channel_id=1, source_target_pairs={{4,0},{8,4},{12,8},{16,12},{20,16},{24,20},{28,24},{32,28},{36,32}... | collective-permute-start | bytes 663560 | tf_op jit(solution)/shard_map/ppermute | solution.py:28
  23.7 3.1 %collective-permute-start.2 = (f32[27,6,1,128]{3,2,1,0:T(1,128)S(1)}, f32[27,6,1,128]{3,2,1,0:T(1,128)S(1)}, u32[]{:S(2)}, u32[]{:S(2)}) collective-permute-start(f32[27,6,1,128]{3,2,1,0:T(1,128)S(1)} %get-tuple-element.104), channel_id=1, source_target_pairs={{0,1},{1,2},{2,3},{3,0},{4,5},{5,6},{6,7},{7,4},{8,9},{9,10},{10,1... | collective-permute-start | bytes 248840 | tf_op jit(solution)/shard_map/ppermute | solution.py:27
  25.3 3.9 %collective-permute-start.3 = (f32[27,6,1,128]{3,2,1,0:T(1,128)S(1)}, f32[27,6,1,128]{3,2,1,0:T(1,128)S(1)}, u32[]{:S(2)}, u32[]{:S(2)}) collective-permute-start(f32[27,6,1,128]{3,2,1,0:T(1,128)S(1)} %get-tuple-element.105), channel_id=1, source_target_pairs={{1,0},{2,1},{3,2},{0,3},{5,4},{6,5},{7,6},{4,7},{9,8},{10,9},{11,1... | collective-permute-start | bytes 248840 | tf_op jit(solution)/shard_map/ppermute | solution.py:28
  44.9 2.0 %copy-start.2 = (f32[4,16,128]{2,1,0:T(8,128)S(1)}, f32[4,16,128]{2,1,0:T(8,128)}, u32[]{:S(2)}) copy-start(f32[4,16,128]{2,1,0:T(8,128)} %pad_maximum_fusion.14) | copy-start | bytes 98308
  44.9 1.9 %copy-start.3 = (f32[4,16,128]{2,1,0:T(8,128)S(1)}, f32[4,16,128]{2,1,0:T(8,128)}, u32[]{:S(2)}) copy-start(f32[4,16,128]{2,1,0:T(8,128)} %pad_maximum_fusion.15) | copy-start | bytes 98308
  45.0 1.9 %copy-start.4 = (f32[4,16,128]{2,1,0:T(8,128)S(1)}, f32[4,16,128]{2,1,0:T(8,128)}, u32[]{:S(2)}) copy-start(f32[4,16,128]{2,1,0:T(8,128)} %pad_maximum_fusion.12) | copy-start | bytes 98308
  45.0 1.9 %copy-start.5 = (f32[4,16,128]{2,1,0:T(8,128)S(1)}, f32[4,16,128]{2,1,0:T(8,128)}, u32[]{:S(2)}) copy-start(f32[4,16,128]{2,1,0:T(8,128)} %pad_maximum_fusion.13) | copy-start | bytes 98308
  45.0 1.9 %copy-start.6 = (f32[4,16,128]{2,1,0:T(8,128)S(1)}, f32[4,16,128]{2,1,0:T(8,128)}, u32[]{:S(2)}) copy-start(f32[4,16,128]{2,1,0:T(8,128)} %pad_maximum_fusion.10) | copy-start | bytes 98308
  45.0 1.9 %copy-start.7 = (f32[4,16,128]{2,1,0:T(8,128)S(1)}, f32[4,16,128]{2,1,0:T(8,128)}, u32[]{:S(2)}) copy-start(f32[4,16,128]{2,1,0:T(8,128)} %pad_maximum_fusion.11) | copy-start | bytes 98308
  45.0 1.9 %copy-start.8 = (f32[4,16,128]{2,1,0:T(8,128)S(1)}, f32[4,16,128]{2,1,0:T(8,128)}, u32[]{:S(2)}) copy-start(f32[4,16,128]{2,1,0:T(8,128)} %pad_maximum_fusion.8) | copy-start | bytes 98308
  45.0 1.9 %copy-start.9 = (f32[4,16,128]{2,1,0:T(8,128)S(1)}, f32[4,16,128]{2,1,0:T(8,128)}, u32[]{:S(2)}) copy-start(f32[4,16,128]{2,1,0:T(8,128)} %pad_maximum_fusion.9) | copy-start | bytes 98308
  45.0 1.9 %copy-start.10 = (f32[4,16,128]{2,1,0:T(8,128)S(1)}, f32[4,16,128]{2,1,0:T(8,128)}, u32[]{:S(2)}) copy-start(f32[4,16,128]{2,1,0:T(8,128)} %pad_maximum_fusion.6) | copy-start | bytes 98308
  45.0 1.9 %copy-start.11 = (f32[4,16,128]{2,1,0:T(8,128)S(1)}, f32[4,16,128]{2,1,0:T(8,128)}, u32[]{:S(2)}) copy-start(f32[4,16,128]{2,1,0:T(8,128)} %pad_maximum_fusion.7) | copy-start | bytes 98308
  45.0 1.9 %copy-start.12 = (f32[4,16,128]{2,1,0:T(8,128)S(1)}, f32[4,16,128]{2,1,0:T(8,128)}, u32[]{:S(2)}) copy-start(f32[4,16,128]{2,1,0:T(8,128)} %pad_maximum_fusion.4) | copy-start | bytes 98308
  45.1 1.9 %copy-start.13 = (f32[4,16,128]{2,1,0:T(8,128)S(1)}, f32[4,16,128]{2,1,0:T(8,128)}, u32[]{:S(2)}) copy-start(f32[4,16,128]{2,1,0:T(8,128)} %pad_maximum_fusion.5) | copy-start | bytes 98308
  45.1 1.9 %copy-start.14 = (f32[4,16,128]{2,1,0:T(8,128)S(1)}, f32[4,16,128]{2,1,0:T(8,128)}, u32[]{:S(2)}) copy-start(f32[4,16,128]{2,1,0:T(8,128)} %pad_maximum_fusion.2) | copy-start | bytes 98308
  45.1 1.9 %copy-start.15 = (f32[4,16,128]{2,1,0:T(8,128)S(1)}, f32[4,16,128]{2,1,0:T(8,128)}, u32[]{:S(2)}) copy-start(f32[4,16,128]{2,1,0:T(8,128)} %pad_maximum_fusion.3) | copy-start | bytes 98308
  45.1 1.9 %copy-start.16 = (f32[8192]{0:T(1024)S(1)}, f32[8192]{0:T(1024)}, u32[]{:S(2)}) copy-start(f32[8192]{0:T(1024)} %get-tuple-element.10) | copy-start | bytes 98308
  45.1 1.9 %copy-start.17 = (f32[8192]{0:T(1024)S(1)}, f32[8192]{0:T(1024)}, u32[]{:S(2)}) copy-start(f32[8192]{0:T(1024)} %get-tuple-element.11) | copy-start | bytes 98308
  45.1 1.9 %copy-start.18 = (f32[8192]{0:T(1024)S(1)}, f32[8192]{0:T(1024)}, u32[]{:S(2)}) copy-start(f32[8192]{0:T(1024)} %get-tuple-element.8) | copy-start | bytes 98308
  45.1 1.9 %copy-start.19 = (f32[8192]{0:T(1024)S(1)}, f32[8192]{0:T(1024)}, u32[]{:S(2)}) copy-start(f32[8192]{0:T(1024)} %get-tuple-element.9) | copy-start | bytes 98308
  45.1 2.1 %copy-start.23 = (f32[27,27]{1,0:T(8,128)S(1)}, f32[27,27]{1,0:T(8,128)}, u32[]{:S(2)}) copy-start(f32[27,27]{1,0:T(8,128)} %copy-done.22) | copy-start | bytes 8752
  45.1 2.1 %copy-start.27 = (pred[8192]{0:T(1024)(128)(4,1)S(1)}, pred[8192]{0:T(1024)(128)(4,1)}, u32[]{:S(2)}) copy-start(pred[8192]{0:T(1024)(128)(4,1)} %copy-done.26) | copy-start | bytes 24580
  45.1 2.1 %copy-start.35 = (f32[27]{0:T(128)S(1)}, f32[27]{0:T(128)}, u32[]{:S(2)}) copy-start(f32[27]{0:T(128)} %constant.61.clone) | copy-start | bytes 328
  45.2 2.1 %copy-start.37 = (f32[27]{0:T(128)S(1)}, f32[27]{0:T(128)}, u32[]{:S(2)}) copy-start(f32[27]{0:T(128)} %constant.62.clone) | copy-start | bytes 328
  45.2 2.0 %copy-start.39 = (f32[27]{0:T(128)S(1)}, f32[27]{0:T(128)}, u32[]{:S(2)}) copy-start(f32[27]{0:T(128)} %constant.63.clone) | copy-start | bytes 328
  45.2 2.0 %copy-start.41 = (f32[27]{0:T(128)S(1)}, f32[27]{0:T(128)}, u32[]{:S(2)}) copy-start(f32[27]{0:T(128)} %constant.64.clone) | copy-start | bytes 328
  49.1 0.7 copy-start.42
  49.2 13.3 %collective-permute-start.4 = (f32[27,1,16,128]{3,2,1,0:T(8,128)S(1)}, f32[27,1,16,128]{3,2,1,0:T(8,128)S(1)}, u32[]{:S(2)}, u32[]{:S(2)}) collective-permute-start(f32[27,1,16,128]{3,2,1,0:T(8,128)S(1)} %get-tuple-element.107), channel_id=1, source_target_pairs={{0,4},{4,8},{8,12},{12,16},{16,20},{20,24},{24,28},{28,32},{32,36}... | collective-permute-start | bytes 663560 | tf_op jit(solution)/shard_map/ppermute | solution.py:27
  50.3 12.7 %collective-permute-start.5 = (f32[27,1,16,128]{3,2,1,0:T(8,128)S(1)}, f32[27,1,16,128]{3,2,1,0:T(8,128)S(1)}, u32[]{:S(2)}, u32[]{:S(2)}) collective-permute-start(f32[27,1,16,128]{3,2,1,0:T(8,128)S(1)} %get-tuple-element.106), channel_id=1, source_target_pairs={{4,0},{8,4},{12,8},{16,12},{20,16},{24,20},{28,24},{32,28},{36,32}... | collective-permute-start | bytes 663560 | tf_op jit(solution)/shard_map/ppermute | solution.py:28
  63.1 2.1 %collective-permute-start.6 = (f32[27,6,1,128]{3,2,1,0:T(1,128)S(1)}, f32[27,6,1,128]{3,2,1,0:T(1,128)S(1)}, u32[]{:S(2)}, u32[]{:S(2)}) collective-permute-start(f32[27,6,1,128]{3,2,1,0:T(1,128)S(1)} %get-tuple-element.102), channel_id=1, source_target_pairs={{0,1},{1,2},{2,3},{3,0},{4,5},{5,6},{6,7},{7,4},{8,9},{9,10},{10,1... | collective-permute-start | bytes 248840 | tf_op jit(solution)/shard_map/ppermute | solution.py:27
  63.7 3.9 %collective-permute-start.7 = (f32[27,6,1,128]{3,2,1,0:T(1,128)S(1)}, f32[27,6,1,128]{3,2,1,0:T(1,128)S(1)}, u32[]{:S(2)}, u32[]{:S(2)}) collective-permute-start(f32[27,6,1,128]{3,2,1,0:T(1,128)S(1)} %get-tuple-element.103), channel_id=1, source_target_pairs={{1,0},{2,1},{3,2},{0,3},{5,4},{6,5},{7,6},{4,7},{9,8},{10,9},{11,1... | collective-permute-start | bytes 248840 | tf_op jit(solution)/shard_map/ppermute | solution.py:28
  70.4 30.6 %copy-start.1 = (f32[9,3,4,16,128]{4,3,2,1,0:T(8,128)}, f32[9,3,4,16,128]{4,3,2,1,0:T(8,128)S(1)}, u32[]{:S(2)}) copy-start(f32[9,3,4,16,128]{4,3,2,1,0:T(8,128)S(1)} %fusion.86) | copy-start | bytes 2654212
  123.2 0.7 copy-start.30
  124.0 0.7 copy-start.20
  124.0 0.7 copy-start.21
  124.1 1.6 copy-start.28
  124.1 1.6 copy-start.31
  124.1 1.6 copy-start.33
where the time goes:
time: 172 us
  local copies, waits for them, and re-layouts  74.6 us (43%)
  blocking collectives  37 us (22%)
  other arithmetic  20.1 us (12%)
  starting transfers between devices  19.8 us (12%)
  waiting for transfers between devices  12 us (7%)
  matrix products  5.55 us (3%)
  between operations  2.62 us (2%)
    all_to_all x1, blocking collectives, per_device(): lax.all_to_all(outgoing.reshape(device_count, CAP, block_size), ('stream'...  37 us
    another operation x1, local copies, waits for them, and re-layouts, per_device(): current.reshape(27, bricks_x, BRICK, bricks_y, BRICK, bricks_z, BRICK)  30.6 us
    transpose x1, local copies, waits for them, and re-layouts, per_device(): brick_table.transpose(1, 3, 5, 0, 2, 4, 6)  17.3 us
    ppermute x4, starting transfers between devices, extended(): after = lax.ppermute(initial, axis, down)  15.3 us
    ppermute x4, waiting for transfers between devices, extended(): before = lax.ppermute(last, axis, up)  6.87 us
    unnamed x101, local copies, waits for them, and re-layouts  6.65 us
    ppermute x4, waiting for transfers between devices, extended(): after = lax.ppermute(initial, axis, down)  5.14 us
    concatenate x9, other arithmetic, roll_span(): jnp.roll(grouped_z[2], 1, axis=-1)  5.01 us
  transfers between devices with their start and end apart: 8, of which 7 were waited for; matrix products, arithmetic and copies ran while one was open for 3% of the time, Pallas kernels for 0%

commit v1 on v0

v1 whole, which is shorter than its diff:
```python
import itertools
import random

import jax
import jax.numpy as jnp
import numpy as np
from jax import lax
from jax.experimental import pallas as pl
from jax.experimental.pallas import tpu as pltpu
from jax.sharding import PartitionSpec as P

MESH = pl.DeviceIdType.MESH
F32 = jnp.float32
BF16 = jnp.bfloat16

N_STREAM = 32
N_DEPTH = 4
N_DEV = N_STREAM * N_DEPTH
CX = 4
CY = 16
NZ = 128
TOP = 8
CHUNKS = 28

line = np.array([1.0 / 6.0, 2.0 / 3.0, 1.0 / 6.0])
power_table = np.array([[1.0, 1.0, 1.0], [-1.0, 0.0, 1.0], [1.0, 0.0, 1.0]])
VELOCITIES = list(itertools.product(range(3), repeat=3))


def equilibrium_terms():
    rows = []
    for a, b, c in VELOCITIES:
        w = line[a] * line[b] * line[c]
        x, y, z = a - 1.0, b - 1.0, c - 1.0
        square = [4.5 * x * x - 1.5, 4.5 * y * y - 1.5, 4.5 * z * z - 1.5]
        rows.append([w * t for t in [1.0, 3 * x, 3 * y, 3 * z] + square + [9 * x * y, 9 * x * z, 9 * y * z]])
    rows = np.array(rows)
    moments = np.kron(np.kron(power_table, power_table), power_table) @ rows
    return rows, np.where(np.abs(moments) < 1e-12, 0.0, moments)


GEQ_TERMS, MOMENT_TERMS = equilibrium_terms()


def combine(coefficients, basis):
    groups = {}
    for value, term in zip(coefficients, basis):
        if value != 0.0:
            groups.setdefault(round(float(value), 12), []).append(term)
    total = None
    for value, terms in groups.items():
        part = terms[0]
        for term in terms[1:]:
            part = part + term
        if value != 1.0:
            part = part * np.float32(value)
        total = part if total is None else total + part
    return total


def along(values, step):
    for axis in (2, 1, 0):
        out = {}
        for key in values:
            if key[axis] == 0:
                keys = [key[:axis] + (j,) + key[axis + 1:] for j in range(3)]
                for k, v in zip(keys, step(*[values[k] for k in keys])):
                    out[k] = v
        values = out
    return values


def to_moments(f0, f1, f2):
    ends = f0 + f2
    return ends + f1, f2 - f0, ends


def from_moments(m0, h1, h2):
    return h2 - h1, m0 - (h2 + h2), h2 + h1


def collide(f, solid, rate):
    moments = along(dict(zip(VELOCITIES, f)), to_moments)
    rho, jx, jy, jz = moments[0, 0, 0], moments[1, 0, 0], moments[0, 1, 0], moments[0, 0, 1]
    inverse = 1.0 / rho
    ux, uy, uz = jx * inverse, jy * inverse, jz * inverse
    basis = [rho, rho * ux, rho * uy, rho * uz, jx * ux, jy * uy, jz * uz, jx * uy, jx * uz, jy * uz]
    change = {}
    for k, key in enumerate(VELOCITIES):
        balance = combine(MOMENT_TERMS[k], basis)
        excess = moments[key] if balance is None else moments[key] - balance
        change[key] = excess * rate(k)
    change = along(change, from_moments)
    return [jnp.where(solid, f[26 - i], f[i] - change[key]) for i, key in enumerate(VELOCITIES)]


def rescaled(f, factors):
    rho = f[0]
    for value in f[1:]:
        rho = rho + value
    speeds = []
    for axis in range(3):
        up = [f[i] for i, v in enumerate(VELOCITIES) if v[axis] == 2]
        down = [f[i] for i, v in enumerate(VELOCITIES) if v[axis] == 0]
        total = up[0]
        for value in up[1:]:
            total = total + value
        for value in down:
            total = total - value
        speeds.append(total)
    inverse = 1.0 / rho
    jx, jy, jz = speeds
    ux, uy, uz = jx * inverse, jy * inverse, jz * inverse
    xx, yy, zz = jx * ux, jy * uy, jz * uz
    still = rho - 1.5 * (xx + yy + zz)
    out = [[None] * 27 for _ in factors]
    for i in range(14):
        a, b, c = (v - 1 for v in VELOCITIES[i])
        weight = np.float32(np.prod([line[v] for v in VELOCITIES[i]]))
        even, odd = still, None
        flow = None
        for sign, j, u in ((a, jx, ux), (b, jy, uy), (c, jz, uz)):
            if sign:
                flow = ((j, u) if sign > 0 else (-j, -u)) if flow is None else (
                    (flow[0] + j, flow[1] + u) if sign > 0 else (flow[0] - j, flow[1] - u))
        if flow is not None:
            even = still + 4.5 * (flow[0] * flow[1])
            odd = (3.0 * weight) * flow[0]
        even = even * weight
        for n, balance in ((i, even if odd is None else even + odd), (26 - i, even if odd is None else even - odd)):
            off = f[n] - balance
            for level, factor in enumerate(factors):
                out[level][n] = balance + factor * off
    return out


def offsets():
    every = [o for o in itertools.product(range(4), range(4), range(4), range(2)) if any(o)]
    random.Random(1).shuffle(every)
    return every


def advance(pop_ref, rates_ref, solid_ref, owners_ref, bricks_ref, levels_ref, adv_ref, got_ref,
            coll0, coll1, final, mask_ref, pick, fine, table_hi, table_lo, out_buf,
            halo_send, halo_recv, adv_sem, far_send, far_recv):
    s, p = lax.axis_index("stream"), lax.axis_index("depth")
    me = s * N_DEPTH + p
    x, y, z, core = s % 4, (s // 16) * 2 + p // 2, (s // 4) % 4, p % 2

    def place(offset):
        tx, ty, tz, tc = (x + offset[0]) % 4, (y + offset[1]) % 4, (z + offset[2]) % 4, (core + offset[3]) % 2
        return (ty // 2) * 16 + tz * 4 + tx, (ty % 2) * 2 + tc

    barrier = pltpu.get_barrier_semaphore()
    for offset in FAR:
        pl.semaphore_signal(barrier, inc=1, device_id=place(offset), device_id_type=MESH)

    spread = (lax.broadcasted_iota(jnp.int32, (32, NZ), 1) // 4 == lax.broadcasted_iota(jnp.int32, (32, NZ), 0)).astype(BF16)
    by_row = jnp.dot(solid_ref[...].astype(F32).astype(BF16), spread, preferred_element_type=F32)
    row = lax.broadcasted_iota(jnp.int32, (CY, NZ), 0) // 4
    mask = jnp.zeros((CY, NZ), F32)
    for b in range(CY // 4):
        mask = jnp.where(row == b, jnp.broadcast_to(by_row[b:b + 1, :], (CY, NZ)), mask)
    mask_ref[...] = mask

    def rate(k):
        halves = sum(1 for v in VELOCITIES[k] if v > 0)
        return rates_ref[k] * np.float32(0.5 ** halves)

    def moved(source, i, layer, half):
        a, b, c = VELOCITIES[i]
        value = source[a, b, c, layer + 2 - a, pl.ds(TOP + 8 * half + 1 - b, 8), :]
        return value if c == 1 else pltpu.roll(value, (c - 1) % NZ, 1)

    def collide_layer(layer, source, target):
        for half in range(2):
            rows = pl.ds(8 * half, 8)
            if source is None:
                f = [pop_ref[i, layer, rows, :] for i in range(27)]
            else:
                f = [moved(source, i, layer, half) for i in range(27)]
            for v, value in zip(VELOCITIES, collide(f, mask_ref[rows, :] > 0.5, rate)):
                target[v[0], v[1], v[2], layer + 1, pl.ds(TOP + 8 * half, 8), :] = value

    def halo(buf, step, n):
        dx, dy = HALO[n]
        first = {1: 2, -1: 0, 0: slice(None)}
        sx, lx = {1: (CX, 0), -1: (1, CX + 1), 0: (pl.ds(1, CX),) * 2}[dx]
        sy, ly = {1: (TOP + CY - 1, TOP - 1), -1: (TOP, TOP + CY), 0: (pl.ds(TOP, CY),) * 2}[dy]
        part = buf.at[first[dx], first[dy]] if dx and dy else (buf.at[first[dx]] if dx else buf.at[:, first[dy]])
        lead = (slice(None),) * (1 if dx and dy else 2)
        to = ((s + dx + N_STREAM) % N_STREAM, (p + dy + N_DEPTH) % N_DEPTH)
        return pltpu.make_async_remote_copy(
            part.at[lead + (sx, sy)], part.at[lead + (lx, ly)],
            halo_send.at[step, n], halo_recv.at[step, n], device_id=to, device_id_type=MESH)

    def sweep(layers, body):
        def once(t, _):
            body(layers(t))
            return 0
        lax.fori_loop(0, 2, once, 0)

    outer, inner = lambda t: 3 * t, lambda t: 1 + t

    sweep(outer, lambda layer: collide_layer(layer, None, coll0))
    pl.semaphore_wait(barrier, N_DEV - 1)
    for n in SIDE_X:
        halo(coll0, 0, n).start()
    sweep(inner, lambda layer: collide_layer(layer, None, coll0))
    for n in SIDE_Y:
        halo(coll0, 0, n).start()

    owner_row = jnp.broadcast_to(owners_ref[...], (N_DEV, N_DEV))
    owner_col = owner_row.T
    sub = lax.broadcasted_iota(jnp.int32, (N_DEV, N_DEV), 0)
    lane = lax.broadcasted_iota(jnp.int32, (N_DEV, N_DEV), 1)
    rank = jnp.sum(jnp.where((owner_row == owner_col) & (sub < lane), 1.0, 0.0), axis=0, keepdims=True)
    code = (bricks_ref[...] + 128 * levels_ref[...] - 127).astype(F32)
    for slot in range(2):
        named = jnp.where((owner_row == sub) & (rank == slot), jnp.broadcast_to(code, (N_DEV, N_DEV)), 0.0)
        taken = (4.0 * jnp.sum(named, axis=1, keepdims=True) - 4.0).astype(jnp.int32)
        for part in range(8):
            number = lane + 128 * part
            for zz in range(4):
                pick[pl.ds((zz * 2 + slot) * 128, 128), pl.ds(part * 128, 128)] = jnp.where(
                    number == taken + zz, 1.0, 0.0).astype(BF16)
    fine[:, :, pl.ds(432, 16), :] = jnp.zeros((2, 4, 16, NZ), F32)

    for n in SIDE_Y:
        halo(coll0, 0, n).wait_recv()
    sweep(inner, lambda layer: collide_layer(layer, coll0, coll1))
    for n in SIDE_X:
        halo(coll0, 0, n).wait_recv()
    sweep(outer, lambda layer: collide_layer(layer, coll0, coll1))
    for n in SIDE_X + SIDE_Y:
        halo(coll1, 1, n).start()

    tau = 1.0 / jnp.full((8, NZ), rates_ref[12], F32)
    factors = [(0.5 + h * (tau - 0.5)) / (h * tau) for h in (2.0, 4.0)]

    def finish(layer):
        for half in range(2):
            f = [moved(coll1, i, layer, half) for i in range(27)]
            for i in range(27):
                final[i, layer, pl.ds(8 * half, 8), :] = f[i]
            for level, values in enumerate(rescaled(f, factors)):
                for i in range(27):
                    for quarter in range(2):
                        fine[level, 2 * half + quarter, pl.ds(i * 16 + layer * 4, 4), :] = values[i][4 * quarter:4 * quarter + 4]

    for n in SIDE_Y:
        halo(coll1, 1, n).wait_recv()
    for layer in (1, 2):
        finish(layer)
    for n in SIDE_X:
        halo(coll1, 1, n).wait_recv()
    for layer in (0, 3):
        finish(layer)
    keep = pltpu.make_async_copy(final, adv_ref, adv_sem)
    keep.start()

    def far(part, offset):
        to = place(offset)
        return pltpu.make_async_remote_copy(
            out_buf.at[PARTS[part], to[0] * N_DEPTH + to[1]], got_ref.at[PARTS[part], me],
            far_send.at[part], far_recv.at[part], device_id=to, device_id_type=MESH)

    half_lane = lax.broadcasted_iota(jnp.int32, (N_DEV, 128), 1) < 64
    for part in range(4):
        if part < 3:
            rows = [pl.ds(part * 128, 128)]
        else:
            rows = [pl.ds(384, 64), pl.ds(384, 64)]
        highs, lows = [], []
        for piece in rows:
            high, low = [], []
            for level in range(2):
                for b in range(4):
                    value = fine[level, b, piece, :]
                    top = value.astype(BF16)
                    high.append(top)
                    low.append((value - top.astype(F32)).astype(BF16))
            highs.append(jnp.concatenate(high, axis=1))
            lows.append(jnp.concatenate(low, axis=1))
        table_hi[...] = jnp.concatenate(highs, axis=0)
        table_lo[...] = jnp.concatenate(lows, axis=0)
        dims = (((1,), (1,)), ((), ()))
        got = lax.dot_general(pick[...], table_hi[...], dims, preferred_element_type=F32)
        got = got + lax.dot_general(pick[...], table_lo[...], dims, preferred_element_type=F32)
        got = got.reshape(4, 2, N_DEV, 128)
        if part < 3:
            out_buf[pl.ds(part * 8, 8)] = got.reshape(8, N_DEV, 128)
        else:
            for zz in range(4):
                out_buf[24 + zz] = jnp.where(half_lane, got[zz, 0], got[zz, 1])
        for offset in FAR:
            far(part, offset).start()
        pltpu.make_async_copy(out_buf.at[PARTS[part], me], got_ref.at[PARTS[part], me], far_recv.at[part]).start()

    for step, buf in enumerate((coll0, coll1)):
        for n in SIDE_X + SIDE_Y:
            halo(buf, step, n).wait_send()
    keep.wait()
    for part in range(4):
        pltpu.make_async_copy(out_buf.at[PARTS[part]], got_ref.at[PARTS[part]], far_recv.at[part]).wait()
        rest = pl.ds(0, N_DEV - 1)
        pltpu.make_async_copy(out_buf.at[PARTS[part], rest], got_ref.at[PARTS[part], rest], far_send.at[part]).wait()


FAR = offsets()
HALO = [(1, 0), (-1, 0), (1, 1), (1, -1), (-1, 1), (-1, -1), (0, 1), (0, -1)]
SIDE_X = [0, 1, 2, 3, 4, 5]
SIDE_Y = [6, 7]
PARTS = [pl.ds(0, 8), pl.ds(8, 8), pl.ds(16, 8), pl.ds(24, 4)]


def arrange(adv_ref, got_ref, adv_out, ghosts_ref, sem):
    keep = pltpu.make_async_copy(adv_ref, adv_out, sem)
    keep.start()
    for part in range(4):
        for zz in range(4):
            for slot in range(2):
                base = slot * 1728 + part * 512 + zz
                if part < 3:
                    turned = got_ref[part * 8 + zz * 2 + slot].T
                    ghosts_ref[pl.ds(base, 128, stride=4), :] = turned
                elif slot == 0:
                    turned = got_ref[24 + zz].T
                    ghosts_ref[pl.ds(base, 48, stride=4), :] = turned[0:48]
                    ghosts_ref[pl.ds(base + 1728, 48, stride=4), :] = turned[64:112]
    keep.wait()


def per_device(populations, moment_rates, solid_bricks, owners, bricks, levels):
    vmem, hbm, smem = (pl.BlockSpec(memory_space=space) for space in (pltpu.VMEM, pl.ANY, pltpu.SMEM))
    padded = (3, 3, 3, CX + 2, CY + 16, NZ)
    adv, got = pl.pallas_call(
        advance,
        out_shape=(jax.ShapeDtypeStruct((27, CX, CY, NZ), F32), jax.ShapeDtypeStruct((CHUNKS, N_DEV, 128), F32)),
        in_specs=[vmem, smem, vmem, vmem, vmem, vmem],
        out_specs=(hbm, hbm),
        scratch_shapes=[
            pltpu.VMEM(padded, F32),
            pltpu.VMEM(padded, F32),
            pltpu.VMEM((27, CX, CY, NZ), F32),
            pltpu.VMEM((CY, NZ), F32),
            pltpu.VMEM((1024, 1024), BF16),
            pltpu.VMEM((2, 4, 448, NZ), F32),
            pltpu.VMEM((128, 1024), BF16),
            pltpu.VMEM((128, 1024), BF16),
            pltpu.VMEM((CHUNKS, N_DEV, 128), F32),
            pltpu.SemaphoreType.DMA((2, 8)),
            pltpu.SemaphoreType.DMA((2, 8)),
            pltpu.SemaphoreType.DMA,
            pltpu.SemaphoreType.DMA((4,)),
            pltpu.SemaphoreType.DMA((4,)),
        ],
        compiler_params=pltpu.CompilerParams(collective_id=0, has_side_effects=True, vmem_limit_bytes=40 << 20),
        name="advance",
    )(populations, moment_rates, solid_bricks.reshape(4, 32), owners.reshape(1, 128), bricks.reshape(1, 128), levels.reshape(1, 128))
    adv, ghosts = pl.pallas_call(
        arrange,
        out_shape=(jax.ShapeDtypeStruct((27, CX, CY, NZ), F32), jax.ShapeDtypeStruct((2 * 1728, N_DEV), F32)),
        in_specs=[hbm, vmem],
        out_specs=(hbm, vmem),
        scratch_shapes=[pltpu.SemaphoreType.DMA],
        compiler_params=pltpu.CompilerParams(vmem_limit_bytes=16 << 20),
        name="arrange",
    )(adv, got)
    return adv, ghosts.reshape(2, 1728, N_DEV).transpose(2, 0, 1)


def solution(mesh):
    return jax.shard_map(
        per_device,
        mesh=mesh,
        in_specs=(
            P(None, "stream", "depth", None),
            P(),
            P("stream", "depth", None),
            P(("stream", "depth"), None),
            P(("stream", "depth")),
            P(("stream", "depth")),
        ),
        out_specs=(P(None, "stream", "depth", None), P(("stream", "depth"), None, None)),
        check_vma=False,
    )
```

time: 172 us -> 57.5 us (0.33)
  local copies, waits for them, and re-layouts: 74.6 us -> 4.46 us
  Pallas kernels: 0 us -> 52.2 us
  blocking collectives: 37 us -> 0 us
  other arithmetic: 20.1 us -> 0 us
  starting transfers between devices: 19.8 us -> 0 us
  waiting for transfers between devices: 12 us -> 0 us
  matrix products: 5.55 us -> 0 us
  between operations: 2.62 us -> 0.65 us
    pallas_call x0 -> x2, Pallas kernels: none -> 52.2 us  [the longest x1 50 us: per_device(): pl.pallas_call(advance, out_shape=(jax.ShapeDtypeStruct((27, CX, CY, NZ),...]
    all_to_all x1 -> x0, blocking collectives: 37 us -> none  [per_device(): lax.all_to_all(outgoing.reshape(device_count, CAP, block_size), ('stream'...]
    another operation x4 -> x0, local copies, waits for them, and re-layouts: 32.7 us -> none  [the longest x1 30.6 us: per_device(): current.reshape(27, bricks_x, BRICK, bricks_y, BRICK, bricks_z, BRICK)]
    ppermute x8 -> x0, starting transfers between devices: 19.8 us -> none  [the longest x4 15.3 us: extended(): after = lax.ppermute(initial, axis, down)]
    transpose x1 -> x0, local copies, waits for them, and re-layouts: 17.3 us -> none  [per_device(): brick_table.transpose(1, 3, 5, 0, 2, 4, 6)]
    ppermute x8 -> x0, waiting for transfers between devices: 12 us -> none  [the longest x4 6.87 us: extended(): before = lax.ppermute(last, axis, up)]
    concatenate x20 -> x0, other arithmetic: 10.6 us -> none  [the longest x9 5.01 us: roll_span(): jnp.roll(grouped_z[2], 1, axis=-1)]
    dot_general x4 -> x0, matrix products: 5.55 us -> none  [the longest x2 3.27 us: collide(): jnp.dot(relaxer, flattened - balance, precision=lax.Precision.HIGHEST)]
  transfers between devices with their start and end apart: 8 -> 0, of which waited for: 7 -> 0; matrix products, arithmetic and copies ran while one was open for 3% -> 0% of each run, Pallas kernels for 0% -> 0%
where the time goes in v1:
time: 57.5 us; the launch traced here: 57.3 us
  Pallas kernels  52.2 us (91%)
  local copies, waits for them, and re-layouts  4.46 us (8%)
  between operations  0.65 us (1%)
    pallas_call x1, Pallas kernels, per_device(): pl.pallas_call(advance, out_shape=(jax.ShapeDtypeStruct((27, CX, CY, NZ),...  50 us
    unnamed x12, local copies, waits for them, and re-layouts  4.46 us
    pallas_call x1, Pallas kernels, per_device(): pl.pallas_call(arrange, out_shape=(jax.ShapeDtypeStruct((27, CX, CY, NZ),...  2.14 us

profile of v1, /device:TPU:1, one launch (start us, length us, event | category | flops | bytes accessed | tf_op | source)
XLA Modules:
  0.0 57.3 jit_solution(17397635016854611009)
XLA Ops:
  0.6 0.0 copy-start
  0.6 1.2 %copy-done = f32[27,4,16,128]{3,2,1,0:T(8,128)S(1)} copy-done((f32[27,4,16,128]{3,2,1,0:T(8,128)S(1)}, f32[27,4,16,128]{3,2,1,0:T(8,128)}, u32[]{:S(2)}) %copy-start) | copy-done | bytes 884760
  1.8 0.0 copy-start.1
  1.8 0.7 %copy-done.1 = s32[1,4,32]{2,1,0:T(4,128)S(1)} copy-done((s32[1,4,32]{2,1,0:T(4,128)S(1)}, s32[1,4,32]{2,1,0:T(4,128)}, u32[]{:S(2)}) %copy-start.1) | copy-done | bytes 536
  2.5 0.0 copy-start.2
  2.5 0.7 %copy-done.2 = f32[27]{0:T(128)S(1)} copy-done((f32[27]{0:T(128)S(1)}, f32[27]{0:T(128)}, u32[]{:S(2)}) %copy-start.2) | copy-done | bytes 132
  3.1 0.0 copy-start.3
  3.1 0.7 %copy-done.3 = s32[128,1]{0,1:T(1,128)S(1)} copy-done((s32[128,1]{0,1:T(1,128)S(1)}, s32[128,1]{0,1:T(1,128)}, u32[]{:S(2)}) %copy-start.3) | copy-done | bytes 536
  3.8 0.0 copy-start.4
  3.8 0.7 %copy-done.4 = s32[128]{0:T(128)S(1)} copy-done((s32[128]{0:T(128)S(1)}, s32[128]{0:T(128)}, u32[]{:S(2)}) %copy-start.4) | copy-done | bytes 536
  4.4 0.0 copy-start.5
  4.5 0.7 %copy-done.5 = s32[128]{0:T(128)S(1)} copy-done((s32[128]{0:T(128)S(1)}, s32[128]{0:T(128)}, u32[]{:S(2)}) %copy-start.5) | copy-done | bytes 536
  5.1 50.0 %advance.1 = (f32[27,4,16,128]{3,2,1,0:T(8,128)S(1)}, f32[28,128,128]{2,1,0:T(8,128)S(1)}) custom-call(f32[27,4,16,128]{3,2,1,0:T(8,128)S(1)} %copy-done, f32[27]{0:T(128)S(1)} %copy-done.2, s32[4,32]{1,0:T(4,128)S(1)} %bitcast.7, s32[1,128]{1,0:T(1,128)S(1)} %bitcast.8, s32[1,128]{1,0:T(1,128)S(1)} %bitcast.9, s32[1,128]{1,0:T(1,128)S(1)} %bitcast.10), custom_call_target="tpu_custom_call" | custom-call | tf_op jit(solution)/shard_map/advance/pallas_call | solution.py:337
  55.1 2.1 %arrange.1 = (f32[27,4,16,128]{3,2,1,0:T(8,128)}, f32[3456,128]{1,0:T(8,128)}) custom-call(f32[27,4,16,128]{3,2,1,0:T(8,128)S(1)} %get-tuple-element.6.adv_ref, f32[28,128,128]{2,1,0:T(8,128)S(1)} %get-tuple-element.7.got_ref), custom_call_target="tpu_custom_call" | custom-call | tf_op jit(solution)/shard_map/arrange/pallas_call | solution.py:361
Async XLA Ops:
  0.6 1.2 %copy-start = (f32[27,4,16,128]{3,2,1,0:T(8,128)S(1)}, f32[27,4,16,128]{3,2,1,0:T(8,128)}, u32[]{:S(2)}) copy-start(f32[27,4,16,128]{3,2,1,0:T(8,128)} %pop_ref.1) | copy-start | bytes 2654212
  1.8 0.7 %copy-start.1 = (s32[1,4,32]{2,1,0:T(4,128)S(1)}, s32[1,4,32]{2,1,0:T(4,128)}, u32[]{:S(2)}) copy-start(s32[1,4,32]{2,1,0:T(4,128)} %param.8) | copy-start | bytes 1540
  2.5 0.7 %copy-start.2 = (f32[27]{0:T(128)S(1)}, f32[27]{0:T(128)}, u32[]{:S(2)}) copy-start(f32[27]{0:T(128)} %rates_ref.1) | copy-start | bytes 328
  3.1 0.7 %copy-start.3 = (s32[128,1]{0,1:T(1,128)S(1)}, s32[128,1]{0,1:T(1,128)}, u32[]{:S(2)}) copy-start(s32[128,1]{0,1:T(1,128)} %param.9) | copy-start | bytes 1540
  3.8 0.7 %copy-start.4 = (s32[128]{0:T(128)S(1)}, s32[128]{0:T(128)}, u32[]{:S(2)}) copy-start(s32[128]{0:T(128)} %param.10) | copy-start | bytes 1540
  4.4 0.7 %copy-start.5 = (s32[128]{0:T(128)S(1)}, s32[128]{0:T(128)}, u32[]{:S(2)}) copy-start(s32[128]{0:T(128)} %param.11) | copy-start | bytes 1540

commit v2 on v1

--- a/solution.py
+++ b/solution.py
@@ -9,7 +9,7 @@
 from jax.experimental.pallas import tpu as pltpu
 from jax.sharding import PartitionSpec as P
 
-MESH = pl.DeviceIdType.MESH
+LOGICAL = pl.DeviceIdType.LOGICAL
 F32 = jnp.float32
 BF16 = jnp.bfloat16
 
@@ -134,27 +134,43 @@
     return out
 
 
-def offsets():
-    every = [o for o in itertools.product(range(4), range(4), range(4), range(2)) if any(o)]
+def hops(k):
+    return sum((0, 1, 2, 1)[part] for part in ((k >> 2) & 3, (k >> 4) & 3, (k >> 1) & 1 | (k >> 5) & 2))
+
+
+def others():
+    every = list(range(1, N_DEV))
     random.Random(1).shuffle(every)
     return every
 
 
-def advance(pop_ref, rates_ref, solid_ref, owners_ref, bricks_ref, levels_ref, adv_ref, got_ref,
+def advance(pop_hbm, rates_hbm, solid_hbm, owners_hbm, bricks_hbm, levels_hbm, adv_ref, got_ref,
+            pop_ref, rates_ref, solid_ref, owners_ref, bricks_ref, levels_ref,
             coll0, coll1, final, mask_ref, pick, fine, table_hi, table_lo, out_buf,
-            halo_send, halo_recv, adv_sem, far_send, far_recv):
+            load_sem, halo_send, halo_recv, adv_sem, far_send, far_recv):
+    loads = [pltpu.make_async_copy(pop_hbm.at[:, layer], pop_ref.at[:, layer], load_sem.at[layer]) for layer in range(CX)]
+    small = [(rates_hbm, rates_ref), (solid_hbm, solid_ref), (owners_hbm, owners_ref), (bricks_hbm, bricks_ref), (levels_hbm, levels_ref)]
+    loads += [pltpu.make_async_copy(a, b, load_sem.at[CX + i]) for i, (a, b) in enumerate(small)]
+    for n in (4, 5, 0, 3, 1, 2, 6, 7, 8):
+        loads[n].start()
     s, p = lax.axis_index("stream"), lax.axis_index("depth")
     me = s * N_DEPTH + p
-    x, y, z, core = s % 4, (s // 16) * 2 + p // 2, (s // 4) % 4, p % 2
-
-    def place(offset):
-        tx, ty, tz, tc = (x + offset[0]) % 4, (y + offset[1]) % 4, (z + offset[2]) % 4, (core + offset[3]) % 2
-        return (ty // 2) * 16 + tz * 4 + tx, (ty % 2) * 2 + tc
+    flips = [(1 << b) * (1 - 2 * ((me // (1 << b)) % 2)) for b in range(7)]
+    low, high = [0], [me]
+    for b in range(3):
+        low = low + [t + flips[b] for t in low]
+    for b in range(3, 7):
+        high = high + [t + flips[b] for t in high]
+
+    def place(k):
+        return high[k >> 3] + low[k & 7]
 
     barrier = pltpu.get_barrier_semaphore()
-    for offset in FAR:
-        pl.semaphore_signal(barrier, inc=1, device_id=place(offset), device_id_type=MESH)
-
+    for k in sorted(FAR, key=lambda k: -hops(k)):
+        pl.semaphore_signal(barrier, inc=1, device_id=place(k), device_id_type=LOGICAL)
+
+    for n in (4, 5):
+        loads[n].wait()
     spread = (lax.broadcasted_iota(jnp.int32, (32, NZ), 1) // 4 == lax.broadcasted_iota(jnp.int32, (32, NZ), 0)).astype(BF16)
     by_row = jnp.dot(solid_ref[...].astype(F32).astype(BF16), spread, preferred_element_type=F32)
     row = lax.broadcasted_iota(jnp.int32, (CY, NZ), 0) // 4
@@ -189,10 +205,10 @@
         sy, ly = {1: (TOP + CY - 1, TOP - 1), -1: (TOP, TOP + CY), 0: (pl.ds(TOP, CY),) * 2}[dy]
         part = buf.at[first[dx], first[dy]] if dx and dy else (buf.at[first[dx]] if dx else buf.at[:, first[dy]])
         lead = (slice(None),) * (1 if dx and dy else 2)
-        to = ((s + dx + N_STREAM) % N_STREAM, (p + dy + N_DEPTH) % N_DEPTH)
+        to = ((s + dx + N_STREAM) % N_STREAM) * N_DEPTH + (p + dy + N_DEPTH) % N_DEPTH
         return pltpu.make_async_remote_copy(
             part.at[lead + (sx, sy)], part.at[lead + (lx, ly)],
-            halo_send.at[step, n], halo_recv.at[step, n], device_id=to, device_id_type=MESH)
+            halo_send.at[step, n], halo_recv.at[step, n], device_id=to, device_id_type=LOGICAL)
 
     def sweep(layers, body):
         def once(t, _):
@@ -202,14 +218,20 @@
 
     outer, inner = lambda t: 3 * t, lambda t: 1 + t
 
+    for n in (0, 3):
+        loads[n].wait()
     sweep(outer, lambda layer: collide_layer(layer, None, coll0))
     pl.semaphore_wait(barrier, N_DEV - 1)
     for n in SIDE_X:
         halo(coll0, 0, n).start()
+    for n in (1, 2):
+        loads[n].wait()
     sweep(inner, lambda layer: collide_layer(layer, None, coll0))
     for n in SIDE_Y:
         halo(coll0, 0, n).start()
 
+    for n in (6, 7, 8):
+        loads[n].wait()
     owner_row = jnp.broadcast_to(owners_ref[...], (N_DEV, N_DEV))
     owner_col = owner_row.T
     sub = lax.broadcasted_iota(jnp.int32, (N_DEV, N_DEV), 0)
@@ -224,7 +246,7 @@
             for zz in range(4):
                 pick[pl.ds((zz * 2 + slot) * 128, 128), pl.ds(part * 128, 128)] = jnp.where(
                     number == taken + zz, 1.0, 0.0).astype(BF16)
-    fine[:, :, pl.ds(432, 16), :] = jnp.zeros((2, 4, 16, NZ), F32)
+    fine[:, :, :, pl.ds(216, 40), :] = jnp.zeros((2, 2, 4, 40, NZ), F32)
 
     for n in SIDE_Y:
         halo(coll0, 0, n).wait_recv()
@@ -238,7 +260,7 @@
     tau = 1.0 / jnp.full((8, NZ), rates_ref[12], F32)
     factors = [(0.5 + h * (tau - 0.5)) / (h * tau) for h in (2.0, 4.0)]
 
-    def finish(layer):
+    def finish(layer, side, which):
         for half in range(2):
             f = [moved(coll1, i, layer, half) for i in range(27)]
             for i in range(27):
@@ -246,56 +268,57 @@
             for level, values in enumerate(rescaled(f, factors)):
                 for i in range(27):
                     for quarter in range(2):
-                        fine[level, 2 * half + quarter, pl.ds(i * 16 + layer * 4, 4), :] = values[i][4 * quarter:4 * quarter + 4]
+                        fine[side, level, 2 * half + quarter, pl.ds(i * 8 + which * 4, 4), :] = values[i][4 * quarter:4 * quarter + 4]
+
+    lanes = lax.broadcasted_iota(jnp.int32, (N_DEV, 128), 1)
+    dims = (((1,), (1,)), ((), ()))
+
+    def send(part):
+        for k in FAR:
+            to = place(k)
+            pltpu.make_async_remote_copy(
+                out_buf.at[PARTS[part], to], got_ref.at[PARTS[part], me],
+                far_send.at[part], far_recv.at[part], device_id=to, device_id_type=LOGICAL).start()
+        pltpu.make_async_copy(out_buf.at[PARTS[part], me], got_ref.at[PARTS[part], me], far_recv.at[part]).start()
+
+    def hand_over(side):
+        for level in range(2):
+            for b in range(4):
+                value = fine[side, level, b]
+                top = value.astype(BF16)
+                columns = pl.ds((level * 4 + b) * NZ, NZ)
+                table_hi[:, columns] = top
+                table_lo[:, columns] = (value - top.astype(F32)).astype(BF16)
+        for pair in range(2):
+            first = 14 * side + 6 * pair
+            for zz in (2 * pair, 2 * pair + 1):
+                chosen = pick[pl.ds(zz * 256, 256), :]
+                got = lax.dot_general(chosen, table_hi[...], dims, preferred_element_type=F32)
+                got = got + lax.dot_general(chosen, table_lo[...], dims, preferred_element_type=F32)
+                slots = [got[0:128], got[128:256]]
+                for slot in range(2):
+                    out_buf[first + 2 * (zz % 2) + slot] = slots[slot][:, 0:128]
+                rest = [value[:, 128:256] for value in slots]
+                out_buf[first + 4 + zz % 2] = jnp.where(lanes < 64, rest[0], pltpu.roll(rest[1], 64, 1))
+                for slot in range(2):
+                    turned = pltpu.roll(rest[slot], (zz * 32 + 64) % 128, 1)
+                    if zz:
+                        turned = jnp.where(lanes // 32 == zz, turned, out_buf[14 * side + 12 + slot])
+                    out_buf[14 * side + 12 + slot] = turned
+            send(2 * side + pair)
 
     for n in SIDE_Y:
         halo(coll1, 1, n).wait_recv()
-    for layer in (1, 2):
-        finish(layer)
+    finish(1, 0, 0)
+    finish(2, 0, 1)
+    hand_over(0)
     for n in SIDE_X:
         halo(coll1, 1, n).wait_recv()
-    for layer in (0, 3):
-        finish(layer)
+    finish(0, 1, 0)
+    finish(3, 1, 1)
     keep = pltpu.make_async_copy(final, adv_ref, adv_sem)
     keep.start()
-
-    def far(part, offset):
-        to = place(offset)
-        return pltpu.make_async_remote_copy(
-            out_buf.at[PARTS[part], to[0] * N_DEPTH + to[1]], got_ref.at[PARTS[part], me],
-            far_send.at[part], far_recv.at[part], device_id=to, device_id_type=MESH)
-
-    half_lane = lax.broadcasted_iota(jnp.int32, (N_DEV, 128), 1) < 64
-    for part in range(4):
-        if part < 3:
-            rows = [pl.ds(part * 128, 128)]
-        else:
-            rows = [pl.ds(384, 64), pl.ds(384, 64)]
-        highs, lows = [], []
-        for piece in rows:
-            high, low = [], []
-            for level in range(2):
-                for b in range(4):
-                    value = fine[level, b, piece, :]
-                    top = value.astype(BF16)
-                    high.append(top)
-                    low.append((value - top.astype(F32)).astype(BF16))
-            highs.append(jnp.concatenate(high, axis=1))
-            lows.append(jnp.concatenate(low, axis=1))
-        table_hi[...] = jnp.concatenate(highs, axis=0)
-        table_lo[...] = jnp.concatenate(lows, axis=0)
-        dims = (((1,), (1,)), ((), ()))
-        got = lax.dot_general(pick[...], table_hi[...], dims, preferred_element_type=F32)
-        got = got + lax.dot_general(pick[...], table_lo[...], dims, preferred_element_type=F32)
-        got = got.reshape(4, 2, N_DEV, 128)
-        if part < 3:
-            out_buf[pl.ds(part * 8, 8)] = got.reshape(8, N_DEV, 128)
-        else:
-            for zz in range(4):
-                out_buf[24 + zz] = jnp.where(half_lane, got[zz, 0], got[zz, 1])
-        for offset in FAR:
-            far(part, offset).start()
-        pltpu.make_async_copy(out_buf.at[PARTS[part], me], got_ref.at[PARTS[part], me], far_recv.at[part]).start()
+    hand_over(1)
 
     for step, buf in enumerate((coll0, coll1)):
         for n in SIDE_X + SIDE_Y:
@@ -307,64 +330,100 @@
         pltpu.make_async_copy(out_buf.at[PARTS[part], rest], got_ref.at[PARTS[part], rest], far_send.at[part]).wait()
 
 
-FAR = offsets()
+FAR = others()
 HALO = [(1, 0), (-1, 0), (1, 1), (1, -1), (-1, 1), (-1, -1), (0, 1), (0, -1)]
 SIDE_X = [0, 1, 2, 3, 4, 5]
 SIDE_Y = [6, 7]
-PARTS = [pl.ds(0, 8), pl.ds(8, 8), pl.ds(16, 8), pl.ds(24, 4)]
-
-
-def arrange(adv_ref, got_ref, adv_out, ghosts_ref, sem):
-    keep = pltpu.make_async_copy(adv_ref, adv_out, sem)
-    keep.start()
+PARTS = [pl.ds(0, 6), pl.ds(6, 8), pl.ds(14, 6), pl.ds(20, 8)]
+
+
+def arrange(adv_ref, got_hbm, adv_out, ghosts_hbm, got_ref, ghosts_ref, kept_ref, keep_sem, load_sem, store_sem):
+    loads = [pltpu.make_async_copy(got_hbm.at[rows], got_ref.at[rows], load_sem.at[part]) for part, rows in enumerate(PARTS)]
+    for load in loads:
+        load.start()
+    fetch = pltpu.make_async_copy(adv_ref, kept_ref, keep_sem.at[0])
+    fetch.start()
+
+    def put(turned, first, slot, velocities, side, zz):
+        for n, i in enumerate(velocities):
+            start, base = first + n * 8, slot * 1728 + i * 64 + zz
+            if side == 0:
+                ghosts_ref[pl.ds(base + 16, 8, stride=4), :] = turned[start:start + 8]
+            else:
+                ghosts_ref[pl.ds(base, 4, stride=4), :] = turned[start:start + 4]
+                ghosts_ref[pl.ds(base + 48, 4, stride=4), :] = turned[start + 4:start + 8]
+
     for part in range(4):
-        for zz in range(4):
+        loads[part].wait()
+        side, pair = part // 2, part % 2
+        first = 14 * side + 6 * pair
+        for zz in (2 * pair, 2 * pair + 1):
             for slot in range(2):
-                base = slot * 1728 + part * 512 + zz
-                if part < 3:
-                    turned = got_ref[part * 8 + zz * 2 + slot].T
-                    ghosts_ref[pl.ds(base, 128, stride=4), :] = turned
-                elif slot == 0:
-                    turned = got_ref[24 + zz].T
-                    ghosts_ref[pl.ds(base, 48, stride=4), :] = turned[0:48]
-                    ghosts_ref[pl.ds(base + 1728, 48, stride=4), :] = turned[64:112]
-    keep.wait()
+                put(got_ref[first + 2 * (zz % 2) + slot].T, 0, slot, range(16), side, zz)
+            turned = got_ref[first + 4 + zz % 2].T
+            for slot in range(2):
+                put(turned, 64 * slot, slot, range(16, 24), side, zz)
+        if pair == 1:
+            for slot in range(2):
+                turned = got_ref[14 * side + 12 + slot].T
+                for zz in range(4):
+                    put(turned, 32 * zz, slot, range(24, 27), side, zz)
+    fetch.wait()
+    stores = [pltpu.make_async_copy(kept_ref, adv_out, keep_sem.at[1]), pltpu.make_async_copy(ghosts_ref, ghosts_hbm, store_sem)]
+    for store in stores:
+        store.start()
+    for store in stores:
+        store.wait()
 
 
 def per_device(populations, moment_rates, solid_bricks, owners, bricks, levels):
-    vmem, hbm, smem = (pl.BlockSpec(memory_space=space) for space in (pltpu.VMEM, pl.ANY, pltpu.SMEM))
+    hbm = pl.BlockSpec(memory_space=pl.ANY)
     padded = (3, 3, 3, CX + 2, CY + 16, NZ)
     adv, got = pl.pallas_call(
         advance,
         out_shape=(jax.ShapeDtypeStruct((27, CX, CY, NZ), F32), jax.ShapeDtypeStruct((CHUNKS, N_DEV, 128), F32)),
-        in_specs=[vmem, smem, vmem, vmem, vmem, vmem],
+        in_specs=[hbm] * 6,
         out_specs=(hbm, hbm),
         scratch_shapes=[
+            pltpu.VMEM((27, CX, CY, NZ), F32),
+            pltpu.SMEM((27,), F32),
+            pltpu.VMEM((4, 32), jnp.int32),
+            pltpu.VMEM((1, 128), jnp.int32),
+            pltpu.VMEM((1, 128), jnp.int32),
+            pltpu.VMEM((1, 128), jnp.int32),
             pltpu.VMEM(padded, F32),
             pltpu.VMEM(padded, F32),
             pltpu.VMEM((27, CX, CY, NZ), F32),
             pltpu.VMEM((CY, NZ), F32),
             pltpu.VMEM((1024, 1024), BF16),
-            pltpu.VMEM((2, 4, 448, NZ), F32),
-            pltpu.VMEM((128, 1024), BF16),
-            pltpu.VMEM((128, 1024), BF16),
+            pltpu.VMEM((2, 2, 4, 256, NZ), F32),
+            pltpu.VMEM((256, 1024), BF16),
+            pltpu.VMEM((256, 1024), BF16),
             pltpu.VMEM((CHUNKS, N_DEV, 128), F32),
+            pltpu.SemaphoreType.DMA((CX + 5,)),
             pltpu.SemaphoreType.DMA((2, 8)),
             pltpu.SemaphoreType.DMA((2, 8)),
             pltpu.SemaphoreType.DMA,
             pltpu.SemaphoreType.DMA((4,)),
             pltpu.SemaphoreType.DMA((4,)),
         ],
-        compiler_params=pltpu.CompilerParams(collective_id=0, has_side_effects=True, vmem_limit_bytes=40 << 20),
+        compiler_params=pltpu.CompilerParams(collective_id=0, has_side_effects=True, vmem_limit_bytes=60 << 20),
         name="advance",
     )(populations, moment_rates, solid_bricks.reshape(4, 32), owners.reshape(1, 128), bricks.reshape(1, 128), levels.reshape(1, 128))
     adv, ghosts = pl.pallas_call(
         arrange,
         out_shape=(jax.ShapeDtypeStruct((27, CX, CY, NZ), F32), jax.ShapeDtypeStruct((2 * 1728, N_DEV), F32)),
-        in_specs=[hbm, vmem],
-        out_specs=(hbm, vmem),
-        scratch_shapes=[pltpu.SemaphoreType.DMA],
-        compiler_params=pltpu.CompilerParams(vmem_limit_bytes=16 << 20),
+        in_specs=[hbm, hbm],
+        out_specs=(hbm, hbm),
+        scratch_shapes=[
+            pltpu.VMEM((CHUNKS, N_DEV, 128), F32),
+            pltpu.VMEM((2 * 1728, N_DEV), F32),
+            pltpu.VMEM((27, CX, CY, NZ), F32),
+            pltpu.SemaphoreType.DMA((2,)),
+            pltpu.SemaphoreType.DMA((4,)),
+            pltpu.SemaphoreType.DMA,
+        ],
+        compiler_params=pltpu.CompilerParams(vmem_limit_bytes=60 << 20),
         name="arrange",
     )(adv, got)
     return adv, ghosts.reshape(2, 1728, N_DEV).transpose(2, 0, 1)

time: 57.5 us -> 48.3 us (0.84); the launches traced: 57.3 us -> 47.5 us
  Pallas kernels: 52.2 us -> 46.8 us
  local copies, waits for them, and re-layouts: 4.46 us -> 0 us
    pallas_call x1, Pallas kernels: 50 us -> 43.5 us  [per_device(): pl.pallas_call(advance, out_shape=(jax.ShapeDtypeStruct((27, CX, CY, NZ),...]
    unnamed x12 -> x0, local copies, waits for them, and re-layouts: 4.46 us -> none
    pallas_call x1, Pallas kernels: 2.14 us -> 3.3 us  [per_device(): pl.pallas_call(arrange, out_shape=(jax.ShapeDtypeStruct((27, CX, CY, NZ),...]
where the time goes in v2:
time: 48.3 us; the launch traced here: 47.5 us
  Pallas kernels  46.8 us (97%)
  between operations  0.64 us (1%)
    pallas_call x1, Pallas kernels, per_device(): pl.pallas_call(advance, out_shape=(jax.ShapeDtypeStruct((27, CX, CY, NZ),...  43.5 us
    pallas_call x1, Pallas kernels, per_device(): pl.pallas_call(arrange, out_shape=(jax.ShapeDtypeStruct((27, CX, CY, NZ),...  3.3 us

profile of v2, /device:TPU:1, one launch (start us, length us, event | category | flops | bytes accessed | tf_op | source)
XLA Modules:
  0.0 47.5 jit_solution(4924403629673022594)
XLA Ops:
  0.6 43.5 %advance.1 = (f32[27,4,16,128]{3,2,1,0:T(8,128)}, f32[28,128,128]{2,1,0:T(8,128)}) custom-call(f32[27,4,16,128]{3,2,1,0:T(8,128)} %pop_hbm.1, f32[27]{0:T(128)} %rates_hbm.1, s32[4,32]{1,0:T(4,128)} %bitcast.7, s32[1,128]{1,0:T(1,128)} %bitcast.8, s32[1,128]{1,0:T(1,128)} %bitcast.9, s32[1,128]{1,0:T(1,128)} %bitcast.10), custom_call_target="tpu_custom_call" | custom-call | tf_op jit(solution)/shard_map/advance/pallas_call | solution.py:382
  44.2 3.3 %arrange.1 = (f32[27,4,16,128]{3,2,1,0:T(8,128)}, f32[3456,128]{1,0:T(8,128)}) custom-call(f32[27,4,16,128]{3,2,1,0:T(8,128)} %get-tuple-element.6.adv_ref, f32[28,128,128]{2,1,0:T(8,128)} %get-tuple-element.7.got_hbm), custom_call_target="tpu_custom_call" | custom-call | tf_op jit(solution)/shard_map/arrange/pallas_call | solution.py:413

commit v3 on v2

--- a/solution.py
+++ b/solution.py
@@ -20,7 +20,7 @@
 CY = 16
 NZ = 128
 TOP = 8
-CHUNKS = 28
+CHUNKS = 27
 
 line = np.array([1.0 / 6.0, 2.0 / 3.0, 1.0 / 6.0])
 power_table = np.array([[1.0, 1.0, 1.0], [-1.0, 0.0, 1.0], [1.0, 0.0, 1.0]])
@@ -177,7 +177,7 @@
     mask = jnp.zeros((CY, NZ), F32)
     for b in range(CY // 4):
         mask = jnp.where(row == b, jnp.broadcast_to(by_row[b:b + 1, :], (CY, NZ)), mask)
-    mask_ref[...] = mask
+    mask_ref[pl.ds(0, CY), :] = mask
 
     def rate(k):
         halves = sum(1 for v in VELOCITIES[k] if v > 0)
@@ -198,17 +198,39 @@
             for v, value in zip(VELOCITIES, collide(f, mask_ref[rows, :] > 0.5, rate)):
                 target[v[0], v[1], v[2], layer + 1, pl.ds(TOP + 8 * half, 8), :] = value
 
-    def halo(buf, step, n):
+    def halo(step, n):
         dx, dy = HALO[n]
-        first = {1: 2, -1: 0, 0: slice(None)}
+        buf, deep = (coll0, 2) if step == 0 else (coll1, 1)
         sx, lx = {1: (CX, 0), -1: (1, CX + 1), 0: (pl.ds(1, CX),) * 2}[dx]
-        sy, ly = {1: (TOP + CY - 1, TOP - 1), -1: (TOP, TOP + CY), 0: (pl.ds(TOP, CY),) * 2}[dy]
-        part = buf.at[first[dx], first[dy]] if dx and dy else (buf.at[first[dx]] if dx else buf.at[:, first[dy]])
-        lead = (slice(None),) * (1 if dx and dy else 2)
+        sy, ly = {1: (TOP + CY - deep, TOP - deep), -1: (TOP, TOP + CY), 0: (TOP,) * 2}[dy]
+        rows = CY if dy == 0 else deep
+        a = {1: pl.ds(2, 1), -1: pl.ds(0, 1), 0: slice(None)}[dx]
+        b = {1: pl.ds(3 - deep, deep), -1: pl.ds(0, deep), 0: slice(None)}[dy]
         to = ((s + dx + N_STREAM) % N_STREAM) * N_DEPTH + (p + dy + N_DEPTH) % N_DEPTH
         return pltpu.make_async_remote_copy(
-            part.at[lead + (sx, sy)], part.at[lead + (lx, ly)],
+            buf.at[a, b, :, sx, pl.ds(sy, rows)], buf.at[a, b, :, lx, pl.ds(ly, rows)],
             halo_send.at[step, n], halo_recv.at[step, n], device_id=to, device_id_type=LOGICAL)
+
+    def mask_row(n):
+        dy = HALO[n][1]
+        to = s * N_DEPTH + (p + dy + N_DEPTH) % N_DEPTH
+        return pltpu.make_async_remote_copy(
+            mask_ref.at[pl.ds(CY - 1 if dy > 0 else 0, 1)], mask_ref.at[pl.ds(CY if dy > 0 else CY + 1, 1)],
+            halo_send.at[1, n], halo_recv.at[1, n], device_id=to, device_id_type=LOGICAL)
+
+    def collide_edges():
+        f = []
+        for a, b, c in VELOCITIES:
+            value = jnp.concatenate(
+                [coll0[a, b, c, layer + 2 - a, pl.ds(TOP - b, 2, stride=CY + 1), :] for layer in range(CX)], axis=0)
+            f.append(value if c == 1 else pltpu.roll(value, (c - 1) % NZ, 1))
+        solid = jnp.concatenate([mask_ref[pl.ds(CY, 2), :]] * CX, axis=0)
+        for (a, b, c), value in zip(VELOCITIES, collide(f, solid > 0.5, rate)):
+            if b != 1:
+                side = 0 if b == 2 else 1
+                for layer in range(CX):
+                    row = 2 * layer + side
+                    coll1[a, b, c, layer + 1, pl.ds(TOP + CY if side else TOP - 1, 1), :] = value[row:row + 1]
 
     def sweep(layers, body):
         def once(t, _):
@@ -223,12 +245,13 @@
     sweep(outer, lambda layer: collide_layer(layer, None, coll0))
     pl.semaphore_wait(barrier, N_DEV - 1)
     for n in SIDE_X:
-        halo(coll0, 0, n).start()
+        halo(0, n).start()
     for n in (1, 2):
         loads[n].wait()
     sweep(inner, lambda layer: collide_layer(layer, None, coll0))
     for n in SIDE_Y:
-        halo(coll0, 0, n).start()
+        mask_row(n).start()
+        halo(0, n).start()
 
     for n in (6, 7, 8):
         loads[n].wait()
@@ -249,13 +272,15 @@
     fine[:, :, :, pl.ds(216, 40), :] = jnp.zeros((2, 2, 4, 40, NZ), F32)
 
     for n in SIDE_Y:
-        halo(coll0, 0, n).wait_recv()
+        mask_row(n).wait_recv()
+        halo(0, n).wait_recv()
     sweep(inner, lambda layer: collide_layer(layer, coll0, coll1))
     for n in SIDE_X:
-        halo(coll0, 0, n).wait_recv()
+        halo(0, n).wait_recv()
     sweep(outer, lambda layer: collide_layer(layer, coll0, coll1))
-    for n in SIDE_X + SIDE_Y:
-        halo(coll1, 1, n).start()
+    for n in SIDE_X:
+        halo(1, n).start()
+    collide_edges()
 
     tau = 1.0 / jnp.full((8, NZ), rates_ref[12], F32)
     factors = [(0.5 + h * (tau - 0.5)) / (h * tau) for h in (2.0, 4.0)]
@@ -290,39 +315,43 @@
                 table_hi[:, columns] = top
                 table_lo[:, columns] = (value - top.astype(F32)).astype(BF16)
         for pair in range(2):
-            first = 14 * side + 6 * pair
+            part = 2 * side + pair
             for zz in (2 * pair, 2 * pair + 1):
                 chosen = pick[pl.ds(zz * 256, 256), :]
                 got = lax.dot_general(chosen, table_hi[...], dims, preferred_element_type=F32)
                 got = got + lax.dot_general(chosen, table_lo[...], dims, preferred_element_type=F32)
-                slots = [got[0:128], got[128:256]]
                 for slot in range(2):
-                    out_buf[first + 2 * (zz % 2) + slot] = slots[slot][:, 0:128]
-                rest = [value[:, 128:256] for value in slots]
-                out_buf[first + 4 + zz % 2] = jnp.where(lanes < 64, rest[0], pltpu.roll(rest[1], 64, 1))
-                for slot in range(2):
-                    turned = pltpu.roll(rest[slot], (zz * 32 + 64) % 128, 1)
-                    if zz:
-                        turned = jnp.where(lanes // 32 == zz, turned, out_buf[14 * side + 12 + slot])
-                    out_buf[14 * side + 12 + slot] = turned
-            send(2 * side + pair)
-
-    for n in SIDE_Y:
-        halo(coll1, 1, n).wait_recv()
+                    value = got[128 * slot:128 * slot + 128]
+                    out_buf[whole(side, zz, slot)] = value[:, 0:128]
+                    place_at = 88 * (side * 8 + zz * 2 + slot)
+                    chunk, start = place_at // 128, place_at % 128
+                    turned = value[:, 128:256]
+                    if start:
+                        turned = pltpu.roll(turned, start, 1)
+                        out_buf[mixed(chunk)] = jnp.where(lanes < start, out_buf[mixed(chunk)], turned)
+                    else:
+                        out_buf[mixed(chunk)] = turned
+                    if start + 88 > 128:
+                        out_buf[mixed(chunk + 1)] = turned
+            send(part)
+
     finish(1, 0, 0)
     finish(2, 0, 1)
     hand_over(0)
     for n in SIDE_X:
-        halo(coll1, 1, n).wait_recv()
+        halo(1, n).wait_recv()
     finish(0, 1, 0)
     finish(3, 1, 1)
     keep = pltpu.make_async_copy(final, adv_ref, adv_sem)
     keep.start()
     hand_over(1)
 
-    for step, buf in enumerate((coll0, coll1)):
-        for n in SIDE_X + SIDE_Y:
-            halo(buf, step, n).wait_send()
+    for n in SIDE_X:
+        halo(0, n).wait_send()
+        halo(1, n).wait_send()
+    for n in SIDE_Y:
+        halo(0, n).wait_send()
+        mask_row(n).wait_send()
     keep.wait()
     for part in range(4):
         pltpu.make_async_copy(out_buf.at[PARTS[part]], got_ref.at[PARTS[part]], far_recv.at[part]).wait()
@@ -334,7 +363,16 @@
 HALO = [(1, 0), (-1, 0), (1, 1), (1, -1), (-1, 1), (-1, -1), (0, 1), (0, -1)]
 SIDE_X = [0, 1, 2, 3, 4, 5]
 SIDE_Y = [6, 7]
-PARTS = [pl.ds(0, 6), pl.ds(6, 8), pl.ds(14, 6), pl.ds(20, 8)]
+FIRST = [0, 6, 13, 20, CHUNKS]
+PARTS = [pl.ds(a, b - a) for a, b in zip(FIRST, FIRST[1:])]
+
+
+def whole(side, zz, slot):
+    return FIRST[2 * side + zz // 2] + zz % 2 * 2 + slot
+
+
+def mixed(n):
+    return ([4, 5] + [10, 11, 12] + [17, 18, 19] + [24, 25, 26])[n]
 
 
 def arrange(adv_ref, got_hbm, adv_out, ghosts_hbm, got_ref, ghosts_ref, kept_ref, keep_sem, load_sem, store_sem):
@@ -344,36 +382,41 @@
     fetch = pltpu.make_async_copy(adv_ref, kept_ref, keep_sem.at[0])
     fetch.start()
 
-    def put(turned, first, slot, velocities, side, zz):
-        for n, i in enumerate(velocities):
-            start, base = first + n * 8, slot * 1728 + i * 64 + zz
-            if side == 0:
-                ghosts_ref[pl.ds(base + 16, 8, stride=4), :] = turned[start:start + 8]
-            else:
-                ghosts_ref[pl.ds(base, 4, stride=4), :] = turned[start:start + 4]
-                ghosts_ref[pl.ds(base + 48, 4, stride=4), :] = turned[start + 4:start + 8]
-
-    for part in range(4):
-        loads[part].wait()
-        side, pair = part // 2, part % 2
-        first = 14 * side + 6 * pair
-        for zz in (2 * pair, 2 * pair + 1):
-            for slot in range(2):
-                put(got_ref[first + 2 * (zz % 2) + slot].T, 0, slot, range(16), side, zz)
-            turned = got_ref[first + 4 + zz % 2].T
-            for slot in range(2):
-                put(turned, 64 * slot, slot, range(16, 24), side, zz)
-        if pair == 1:
-            for slot in range(2):
-                turned = got_ref[14 * side + 12 + slot].T
-                for zz in range(4):
-                    put(turned, 32 * zz, slot, range(24, 27), side, zz)
+    def put(eight, i, side, zz, slot):
+        base = slot * 1728 + i * 64 + zz
+        if side == 0:
+            ghosts_ref[pl.ds(base + 16, 8, stride=4), :] = eight
+        else:
+            ghosts_ref[pl.ds(base, 4, stride=4), :] = eight[0:4]
+            ghosts_ref[pl.ds(base + 48, 4, stride=4), :] = eight[4:8]
+
+    def store(n, first, length):
+        rows = pl.ds(first, length)
+        stores.append(pltpu.make_async_copy(ghosts_ref.at[rows], ghosts_hbm.at[rows], store_sem.at[n]))
+        stores[-1].start()
+
+    for load in loads:
+        load.wait()
+    stores = []
+    for slot in range(2):
+        for side in range(2):
+            for zz in range(4):
+                turned = got_ref[whole(side, zz, slot)].T
+                for i in range(16):
+                    put(turned[8 * i:8 * i + 8], i, side, zz, slot)
+        store(slot, slot * 1728, 1024)
     fetch.wait()
-    stores = [pltpu.make_async_copy(kept_ref, adv_out, keep_sem.at[1]), pltpu.make_async_copy(ghosts_ref, ghosts_hbm, store_sem)]
-    for store in stores:
-        store.start()
-    for store in stores:
-        store.wait()
+    stores.append(pltpu.make_async_copy(kept_ref, adv_out, keep_sem.at[1]))
+    stores[-1].start()
+    for n in range(11):
+        turned = got_ref[mixed(n)].T
+        for row in range(16):
+            entry, i = (16 * n + row) // 11, 16 + (16 * n + row) % 11
+            put(turned[8 * row:8 * row + 8], i, entry // 8, entry % 8 // 2, entry % 2)
+    for slot in range(2):
+        store(2 + slot, slot * 1728 + 1024, 704)
+    for copy in stores:
+        copy.wait()
 
 
 def per_device(populations, moment_rates, solid_bricks, owners, bricks, levels):
@@ -394,7 +437,7 @@
             pltpu.VMEM(padded, F32),
             pltpu.VMEM(padded, F32),
             pltpu.VMEM((27, CX, CY, NZ), F32),
-            pltpu.VMEM((CY, NZ), F32),
+            pltpu.VMEM((CY + 8, NZ), F32),
             pltpu.VMEM((1024, 1024), BF16),
             pltpu.VMEM((2, 2, 4, 256, NZ), F32),
             pltpu.VMEM((256, 1024), BF16),
@@ -421,7 +464,7 @@
             pltpu.VMEM((27, CX, CY, NZ), F32),
             pltpu.SemaphoreType.DMA((2,)),
             pltpu.SemaphoreType.DMA((4,)),
-            pltpu.SemaphoreType.DMA,
+            pltpu.SemaphoreType.DMA((4,)),
         ],
         compiler_params=pltpu.CompilerParams(vmem_limit_bytes=60 << 20),
         name="arrange",

time: 48.3 us -> 45.9 us (0.950); the launches traced: 47.5 us -> 45.8 us
  Pallas kernels: 46.8 us -> 45.1 us
    pallas_call x1, Pallas kernels: 43.5 us -> 41.9 us  [per_device(): pl.pallas_call(advance, out_shape=(jax.ShapeDtypeStruct((27, CX, CY, NZ),...]
where the time goes in v3:
time: 45.9 us; the launch traced here: 45.8 us
  Pallas kernels  45.1 us (98%)
  between operations  0.64 us (1%)
    pallas_call x1, Pallas kernels, per_device(): pl.pallas_call(advance, out_shape=(jax.ShapeDtypeStruct((27, CX, CY, NZ),...  41.9 us
    pallas_call x1, Pallas kernels, per_device(): pl.pallas_call(arrange, out_shape=(jax.ShapeDtypeStruct((27, CX, CY, NZ),...  3.19 us

profile of v3, /device:TPU:1, one launch (start us, length us, event | category | flops | bytes accessed | tf_op | source)
XLA Modules:
  0.0 45.8 jit_solution(6066733285630617531)
XLA Ops:
  0.6 41.9 %advance.1 = (f32[27,4,16,128]{3,2,1,0:T(8,128)}, f32[27,128,128]{2,1,0:T(8,128)}) custom-call(f32[27,4,16,128]{3,2,1,0:T(8,128)} %pop_hbm.1, f32[27]{0:T(128)} %rates_hbm.1, s32[4,32]{1,0:T(4,128)} %bitcast.7, s32[1,128]{1,0:T(1,128)} %bitcast.8, s32[1,128]{1,0:T(1,128)} %bitcast.9, s32[1,128]{1,0:T(1,128)} %bitcast.10), custom_call_target="tpu_custom_call" | custom-call | tf_op jit(solution)/shard_map/advance/pallas_call | solution.py:425
  42.6 3.2 %arrange.1 = (f32[27,4,16,128]{3,2,1,0:T(8,128)}, f32[3456,128]{1,0:T(8,128)}) custom-call(f32[27,4,16,128]{3,2,1,0:T(8,128)} %get-tuple-element.6.adv_ref, f32[27,128,128]{2,1,0:T(8,128)} %get-tuple-element.7.got_hbm), custom_call_target="tpu_custom_call" | custom-call | tf_op jit(solution)/shard_map/arrange/pallas_call | solution.py:456

commit v4 on v3

--- a/solution.py
+++ b/solution.py
@@ -147,7 +147,7 @@
 def advance(pop_hbm, rates_hbm, solid_hbm, owners_hbm, bricks_hbm, levels_hbm, adv_ref, got_ref,
             pop_ref, rates_ref, solid_ref, owners_ref, bricks_ref, levels_ref,
             coll0, coll1, final, mask_ref, pick, fine, table_hi, table_lo, out_buf,
-            load_sem, halo_send, halo_recv, adv_sem, far_send, far_recv):
+            load_sem, halo_send, halo_recv, adv_sem, far_send, far_recv, joined):
     loads = [pltpu.make_async_copy(pop_hbm.at[:, layer], pop_ref.at[:, layer], load_sem.at[layer]) for layer in range(CX)]
     small = [(rates_hbm, rates_ref), (solid_hbm, solid_ref), (owners_hbm, owners_ref), (bricks_hbm, bricks_ref), (levels_hbm, levels_ref)]
     loads += [pltpu.make_async_copy(a, b, load_sem.at[CX + i]) for i, (a, b) in enumerate(small)]
@@ -165,8 +165,13 @@
     def place(k):
         return high[k >> 3] + low[k & 7]
 
+    def beside(dx, dy):
+        return ((s + dx + N_STREAM) % N_STREAM) * N_DEPTH + (p + dy + N_DEPTH) % N_DEPTH
+
     barrier = pltpu.get_barrier_semaphore()
-    for k in sorted(FAR, key=lambda k: -hops(k)):
+    for n in SIDE_X:
+        pl.semaphore_signal(barrier, inc=1, device_id=beside(*HALO[n]), device_id_type=LOGICAL)
+    for k in sorted(PLANE + COLUMN, key=lambda k: -hops(k)):
         pl.semaphore_signal(barrier, inc=1, device_id=place(k), device_id_type=LOGICAL)
 
     for n in (4, 5):
@@ -206,17 +211,15 @@
         rows = CY if dy == 0 else deep
         a = {1: pl.ds(2, 1), -1: pl.ds(0, 1), 0: slice(None)}[dx]
         b = {1: pl.ds(3 - deep, deep), -1: pl.ds(0, deep), 0: slice(None)}[dy]
-        to = ((s + dx + N_STREAM) % N_STREAM) * N_DEPTH + (p + dy + N_DEPTH) % N_DEPTH
         return pltpu.make_async_remote_copy(
             buf.at[a, b, :, sx, pl.ds(sy, rows)], buf.at[a, b, :, lx, pl.ds(ly, rows)],
-            halo_send.at[step, n], halo_recv.at[step, n], device_id=to, device_id_type=LOGICAL)
+            halo_send.at[step, n], halo_recv.at[step, n], device_id=beside(dx, dy), device_id_type=LOGICAL)
 
     def mask_row(n):
         dy = HALO[n][1]
-        to = s * N_DEPTH + (p + dy + N_DEPTH) % N_DEPTH
         return pltpu.make_async_remote_copy(
             mask_ref.at[pl.ds(CY - 1 if dy > 0 else 0, 1)], mask_ref.at[pl.ds(CY if dy > 0 else CY + 1, 1)],
-            halo_send.at[1, n], halo_recv.at[1, n], device_id=to, device_id_type=LOGICAL)
+            halo_send.at[1, n], halo_recv.at[1, n], device_id=beside(0, dy), device_id_type=LOGICAL)
 
     def collide_edges():
         f = []
@@ -243,9 +246,11 @@
     for n in (0, 3):
         loads[n].wait()
     sweep(outer, lambda layer: collide_layer(layer, None, coll0))
-    pl.semaphore_wait(barrier, N_DEV - 1)
+    pl.semaphore_wait(barrier, len(SIDE_X) + len(PLANE) + len(COLUMN))
     for n in SIDE_X:
         halo(0, n).start()
+    for k in sorted(COLUMN, key=lambda k: -hops(k)):
+        pl.semaphore_signal(joined, inc=1, device_id=place(k), device_id_type=LOGICAL)
     for n in (1, 2):
         loads[n].wait()
     sweep(inner, lambda layer: collide_layer(layer, None, coll0))
@@ -337,6 +342,7 @@
 
     finish(1, 0, 0)
     finish(2, 0, 1)
+    pl.semaphore_wait(joined, len(COLUMN))
     hand_over(0)
     for n in SIDE_X:
         halo(1, n).wait_recv()
@@ -360,6 +366,8 @@
 
 
 FAR = others()
+PLANE = [k << 2 for k in range(1, 16)]
+COLUMN = [k for k in range(1, N_DEV) if not k & 60]
 HALO = [(1, 0), (-1, 0), (1, 1), (1, -1), (-1, 1), (-1, -1), (0, 1), (0, -1)]
 SIDE_X = [0, 1, 2, 3, 4, 5]
 SIDE_Y = [6, 7]
@@ -449,6 +457,7 @@
             pltpu.SemaphoreType.DMA,
             pltpu.SemaphoreType.DMA((4,)),
             pltpu.SemaphoreType.DMA((4,)),
+            pltpu.SemaphoreType.REGULAR,
         ],
         compiler_params=pltpu.CompilerParams(collective_id=0, has_side_effects=True, vmem_limit_bytes=60 << 20),
         name="advance",

time: 45.9 us -> 45.2 us (0.985)
  Pallas kernels: 45.1 us -> 44.4 us
    pallas_call x1, Pallas kernels: 41.9 us -> 41.2 us  [per_device(): pl.pallas_call(advance, out_shape=(jax.ShapeDtypeStruct((27, CX, CY, NZ),...]
where the time goes in v4:
time: 45.2 us; the launch traced here: 45 us
  Pallas kernels  44.4 us (98%)
  between operations  0.64 us (1%)
    pallas_call x1, Pallas kernels, per_device(): pl.pallas_call(advance, out_shape=(jax.ShapeDtypeStruct((27, CX, CY, NZ),...  41.2 us
    pallas_call x1, Pallas kernels, per_device(): pl.pallas_call(arrange, out_shape=(jax.ShapeDtypeStruct((27, CX, CY, NZ),...  3.19 us

profile of v4, /device:TPU:1, one launch (start us, length us, event | category | flops | bytes accessed | tf_op | source)
XLA Modules:
  0.0 45.0 jit_solution(5473237548873599815)
XLA Ops:
  0.6 41.2 %advance.1 = (f32[27,4,16,128]{3,2,1,0:T(8,128)}, f32[27,128,128]{2,1,0:T(8,128)}) custom-call(f32[27,4,16,128]{3,2,1,0:T(8,128)} %pop_hbm.1, f32[27]{0:T(128)} %rates_hbm.1, s32[4,32]{1,0:T(4,128)} %bitcast.7, s32[1,128]{1,0:T(1,128)} %bitcast.8, s32[1,128]{1,0:T(1,128)} %bitcast.9, s32[1,128]{1,0:T(1,128)} %bitcast.10), custom_call_target="tpu_custom_call" | custom-call | tf_op jit(solution)/shard_map/advance/pallas_call | solution.py:433
  41.8 3.2 %arrange.1 = (f32[27,4,16,128]{3,2,1,0:T(8,128)}, f32[3456,128]{1,0:T(8,128)}) custom-call(f32[27,4,16,128]{3,2,1,0:T(8,128)} %get-tuple-element.6.adv_ref, f32[27,128,128]{2,1,0:T(8,128)} %get-tuple-element.7.got_hbm), custom_call_target="tpu_custom_call" | custom-call | tf_op jit(solution)/shard_map/arrange/pallas_call | solution.py:465

commit v5 on v4

--- a/solution.py
+++ b/solution.py
@@ -141,6 +141,7 @@
 def others():
     every = list(range(1, N_DEV))
     random.Random(1).shuffle(every)
+    every.sort(key=lambda k: -hops(k))
     return every
 
 

time: 45.2 us -> 43.8 us (0.969)
  Pallas kernels: 44.4 us -> 43 us
    pallas_call x1, Pallas kernels: 41.2 us -> 39.8 us  [per_device(): pl.pallas_call(advance, out_shape=(jax.ShapeDtypeStruct((27, CX, CY, NZ),...]
where the time goes in v5:
time: 43.8 us; the launch traced here: 43.7 us
  Pallas kernels  43 us (98%)
  between operations  0.64 us (1%)
    pallas_call x1, Pallas kernels, per_device(): pl.pallas_call(advance, out_shape=(jax.ShapeDtypeStruct((27, CX, CY, NZ),...  39.8 us
    pallas_call x1, Pallas kernels, per_device(): pl.pallas_call(arrange, out_shape=(jax.ShapeDtypeStruct((27, CX, CY, NZ),...  3.19 us

profile of v5, /device:TPU:1, one launch (start us, length us, event | category | flops | bytes accessed | tf_op | source)
XLA Modules:
  0.0 43.7 jit_solution(9801887940945319329)
XLA Ops:
  0.6 39.8 %advance.1 = (f32[27,4,16,128]{3,2,1,0:T(8,128)}, f32[27,128,128]{2,1,0:T(8,128)}) custom-call(f32[27,4,16,128]{3,2,1,0:T(8,128)} %pop_hbm.1, f32[27]{0:T(128)} %rates_hbm.1, s32[4,32]{1,0:T(4,128)} %bitcast.7, s32[1,128]{1,0:T(1,128)} %bitcast.8, s32[1,128]{1,0:T(1,128)} %bitcast.9, s32[1,128]{1,0:T(1,128)} %bitcast.10), custom_call_target="tpu_custom_call" | custom-call | tf_op jit(solution)/shard_map/advance/pallas_call | solution.py:434
  40.5 3.2 %arrange.1 = (f32[27,4,16,128]{3,2,1,0:T(8,128)}, f32[3456,128]{1,0:T(8,128)}) custom-call(f32[27,4,16,128]{3,2,1,0:T(8,128)} %get-tuple-element.6.adv_ref, f32[27,128,128]{2,1,0:T(8,128)} %get-tuple-element.7.got_hbm), custom_call_target="tpu_custom_call" | custom-call | tf_op jit(solution)/shard_map/arrange/pallas_call | solution.py:466

commit v6 on v5

--- a/solution.py
+++ b/solution.py
@@ -281,9 +281,27 @@
         mask_row(n).wait_recv()
         halo(0, n).wait_recv()
     sweep(inner, lambda layer: collide_layer(layer, coll0, coll1))
-    for n in SIDE_X:
-        halo(0, n).wait_recv()
-    sweep(outer, lambda layer: collide_layer(layer, coll0, coll1))
+    from_far = s % 4 == 0
+
+    def arrive(swapped):
+        def wait(dx):
+            for n in SIDE_X:
+                if HALO[n][0] == dx:
+                    halo(0, n).wait_recv()
+
+        @pl.when(from_far != swapped)
+        def _():
+            wait(-1)
+
+        @pl.when(from_far == swapped)
+        def _():
+            wait(1)
+
+    near = jnp.where(from_far, CX - 1, 0)
+    arrive(False)
+    collide_layer(near, coll0, coll1)
+    arrive(True)
+    collide_layer(CX - 1 - near, coll0, coll1)
     for n in SIDE_X:
         halo(1, n).start()
     collide_edges()
@@ -320,26 +338,25 @@
                 columns = pl.ds((level * 4 + b) * NZ, NZ)
                 table_hi[:, columns] = top
                 table_lo[:, columns] = (value - top.astype(F32)).astype(BF16)
-        for pair in range(2):
-            part = 2 * side + pair
-            for zz in (2 * pair, 2 * pair + 1):
-                chosen = pick[pl.ds(zz * 256, 256), :]
-                got = lax.dot_general(chosen, table_hi[...], dims, preferred_element_type=F32)
-                got = got + lax.dot_general(chosen, table_lo[...], dims, preferred_element_type=F32)
-                for slot in range(2):
-                    value = got[128 * slot:128 * slot + 128]
-                    out_buf[whole(side, zz, slot)] = value[:, 0:128]
-                    place_at = 88 * (side * 8 + zz * 2 + slot)
-                    chunk, start = place_at // 128, place_at % 128
-                    turned = value[:, 128:256]
-                    if start:
-                        turned = pltpu.roll(turned, start, 1)
-                        out_buf[mixed(chunk)] = jnp.where(lanes < start, out_buf[mixed(chunk)], turned)
-                    else:
-                        out_buf[mixed(chunk)] = turned
-                    if start + 88 > 128:
-                        out_buf[mixed(chunk + 1)] = turned
-            send(part)
+        for zz in range(4):
+            chosen = pick[pl.ds(zz * 256, 256), :]
+            got = lax.dot_general(chosen, table_hi[...], dims, preferred_element_type=F32)
+            got = got + lax.dot_general(chosen, table_lo[...], dims, preferred_element_type=F32)
+            for slot in range(2):
+                value = got[128 * slot:128 * slot + 128]
+                out_buf[whole(side, zz, slot)] = value[:, 0:128]
+                place_at = 88 * (side * 8 + zz * 2 + slot)
+                chunk, start = place_at // 128, place_at % 128
+                turned = value[:, 128:256]
+                if start:
+                    turned = pltpu.roll(turned, start, 1)
+                    out_buf[mixed(chunk)] = jnp.where(lanes < start, out_buf[mixed(chunk)], turned)
+                else:
+                    out_buf[mixed(chunk)] = turned
+                if start + 88 > 128:
+                    out_buf[mixed(chunk + 1)] = turned
+            if 4 * side + zz in ENDS:
+                send(ENDS.index(4 * side + zz))
 
     finish(1, 0, 0)
     finish(2, 0, 1)
@@ -360,7 +377,7 @@
         halo(0, n).wait_send()
         mask_row(n).wait_send()
     keep.wait()
-    for part in range(4):
+    for part in range(len(PARTS)):
         pltpu.make_async_copy(out_buf.at[PARTS[part]], got_ref.at[PARTS[part]], far_recv.at[part]).wait()
         rest = pl.ds(0, N_DEV - 1)
         pltpu.make_async_copy(out_buf.at[PARTS[part], rest], got_ref.at[PARTS[part], rest], far_send.at[part]).wait()
@@ -372,20 +389,28 @@
 HALO = [(1, 0), (-1, 0), (1, 1), (1, -1), (-1, 1), (-1, -1), (0, 1), (0, -1)]
 SIDE_X = [0, 1, 2, 3, 4, 5]
 SIDE_Y = [6, 7]
-FIRST = [0, 6, 13, 20, CHUNKS]
+ENDS = [1, 3, 7]
+NUMBER = {}
+FIRST = [0]
+for steps in zip([0] + [end + 1 for end in ENDS], ENDS):
+    group = [("whole", step, slot) for step in range(steps[0], steps[1] + 1) for slot in range(2)]
+    group += [("mixed", n) for n in range(176 * steps[0] // 128, 176 * (steps[1] + 1) // 128)]
+    NUMBER.update({name: FIRST[-1] + n for n, name in enumerate(group)})
+    FIRST.append(FIRST[-1] + len(group))
 PARTS = [pl.ds(a, b - a) for a, b in zip(FIRST, FIRST[1:])]
 
 
 def whole(side, zz, slot):
-    return FIRST[2 * side + zz // 2] + zz % 2 * 2 + slot
+    return NUMBER["whole", 4 * side + zz, slot]
 
 
 def mixed(n):
-    return ([4, 5] + [10, 11, 12] + [17, 18, 19] + [24, 25, 26])[n]
+    return NUMBER["mixed", n]
 
 
 def arrange(adv_ref, got_hbm, adv_out, ghosts_hbm, got_ref, ghosts_ref, kept_ref, keep_sem, load_sem, store_sem):
-    loads = [pltpu.make_async_copy(got_hbm.at[rows], got_ref.at[rows], load_sem.at[part]) for part, rows in enumerate(PARTS)]
+    pieces = [pl.ds(0, 6), pl.ds(6, 7), pl.ds(13, 7), pl.ds(20, 7)]
+    loads = [pltpu.make_async_copy(got_hbm.at[rows], got_ref.at[rows], load_sem.at[n]) for n, rows in enumerate(pieces)]
     for load in loads:
         load.start()
     fetch = pltpu.make_async_copy(adv_ref, kept_ref, keep_sem.at[0])
@@ -456,8 +481,8 @@
             pltpu.SemaphoreType.DMA((2, 8)),
             pltpu.SemaphoreType.DMA((2, 8)),
             pltpu.SemaphoreType.DMA,
-            pltpu.SemaphoreType.DMA((4,)),
-            pltpu.SemaphoreType.DMA((4,)),
+            pltpu.SemaphoreType.DMA((len(PARTS),)),
+            pltpu.SemaphoreType.DMA((len(PARTS),)),
             pltpu.SemaphoreType.REGULAR,
         ],
         compiler_params=pltpu.CompilerParams(collective_id=0, has_side_effects=True, vmem_limit_bytes=60 << 20),

time: 43.8 us -> 43.6 us (level)
  no operation moved by 1% of the time
where the time goes in v6:
time: 43.6 us; the launch traced here: 43.4 us
  Pallas kernels  42.8 us (98%)
  between operations  0.64 us (1%)
    pallas_call x1, Pallas kernels, per_device(): pl.pallas_call(advance, out_shape=(jax.ShapeDtypeStruct((27, CX, CY, NZ),...  39.6 us
    pallas_call x1, Pallas kernels, per_device(): pl.pallas_call(arrange, out_shape=(jax.ShapeDtypeStruct((27, CX, CY, NZ),...  3.19 us

profile of v6, /device:TPU:1, one launch (start us, length us, event | category | flops | bytes accessed | tf_op | source)
XLA Modules:
  0.0 43.4 jit_solution(11542722822890940553)
XLA Ops:
  0.6 39.6 %advance.1 = (f32[27,4,16,128]{3,2,1,0:T(8,128)}, f32[27,128,128]{2,1,0:T(8,128)}) custom-call(f32[27,4,16,128]{3,2,1,0:T(8,128)} %pop_hbm.1, f32[27]{0:T(128)} %rates_hbm.1, s32[4,32]{1,0:T(4,128)} %bitcast.7, s32[1,128]{1,0:T(1,128)} %bitcast.8, s32[1,128]{1,0:T(1,128)} %bitcast.9, s32[1,128]{1,0:T(1,128)} %bitcast.10), custom_call_target="tpu_custom_call" | custom-call | tf_op jit(solution)/shard_map/advance/pallas_call | solution.py:459
  40.2 3.2 %arrange.1 = (f32[27,4,16,128]{3,2,1,0:T(8,128)}, f32[3456,128]{1,0:T(8,128)}) custom-call(f32[27,4,16,128]{3,2,1,0:T(8,128)} %get-tuple-element.6.adv_ref, f32[27,128,128]{2,1,0:T(8,128)} %get-tuple-element.7.got_hbm), custom_call_target="tpu_custom_call" | custom-call | tf_op jit(solution)/shard_map/arrange/pallas_call | solution.py:491

commit v7 on v6

--- a/solution.py
+++ b/solution.py
@@ -147,7 +147,7 @@
 
 def advance(pop_hbm, rates_hbm, solid_hbm, owners_hbm, bricks_hbm, levels_hbm, adv_ref, got_ref,
             pop_ref, rates_ref, solid_ref, owners_ref, bricks_ref, levels_ref,
-            coll0, coll1, final, mask_ref, pick, fine, table_hi, table_lo, out_buf,
+            coll0, coll1, final, mask_ref, pick, fine, table, out_buf,
             load_sem, halo_send, halo_recv, adv_sem, far_send, far_recv, joined):
     loads = [pltpu.make_async_copy(pop_hbm.at[:, layer], pop_ref.at[:, layer], load_sem.at[layer]) for layer in range(CX)]
     small = [(rates_hbm, rates_ref), (solid_hbm, solid_ref), (owners_hbm, owners_ref), (bricks_hbm, bricks_ref), (levels_hbm, levels_ref)]
@@ -336,12 +336,11 @@
                 value = fine[side, level, b]
                 top = value.astype(BF16)
                 columns = pl.ds((level * 4 + b) * NZ, NZ)
-                table_hi[:, columns] = top
-                table_lo[:, columns] = (value - top.astype(F32)).astype(BF16)
+                table[:, columns] = top
+                table[:, pl.ds((8 + level * 4 + b) * NZ, NZ)] = (value - top.astype(F32)).astype(BF16)
         for zz in range(4):
             chosen = pick[pl.ds(zz * 256, 256), :]
-            got = lax.dot_general(chosen, table_hi[...], dims, preferred_element_type=F32)
-            got = got + lax.dot_general(chosen, table_lo[...], dims, preferred_element_type=F32)
+            got = lax.dot_general(jnp.concatenate([chosen, chosen], axis=1), table[...], dims, preferred_element_type=F32)
             for slot in range(2):
                 value = got[128 * slot:128 * slot + 128]
                 out_buf[whole(side, zz, slot)] = value[:, 0:128]
@@ -474,8 +473,7 @@
             pltpu.VMEM((CY + 8, NZ), F32),
             pltpu.VMEM((1024, 1024), BF16),
             pltpu.VMEM((2, 2, 4, 256, NZ), F32),
-            pltpu.VMEM((256, 1024), BF16),
-            pltpu.VMEM((256, 1024), BF16),
+            pltpu.VMEM((256, 2048), BF16),
             pltpu.VMEM((CHUNKS, N_DEV, 128), F32),
             pltpu.SemaphoreType.DMA((CX + 5,)),
             pltpu.SemaphoreType.DMA((2, 8)),

time: 43.6 us -> 43.6 us (level)
  no operation moved by 1% of the time
where the time goes in v7:
time: 43.6 us; the launch traced here: 43.4 us
  Pallas kernels  42.8 us (98%)
  between operations  0.64 us (1%)
    pallas_call x1, Pallas kernels, per_device(): pl.pallas_call(advance, out_shape=(jax.ShapeDtypeStruct((27, CX, CY, NZ),...  39.6 us
    pallas_call x1, Pallas kernels, per_device(): pl.pallas_call(arrange, out_shape=(jax.ShapeDtypeStruct((27, CX, CY, NZ),...  3.19 us

profile of v7, /device:TPU:1, one launch (start us, length us, event | category | flops | bytes accessed | tf_op | source)
XLA Modules:
  0.0 43.4 jit_solution(4134286573310948781)
XLA Ops:
  0.6 39.6 %advance.1 = (f32[27,4,16,128]{3,2,1,0:T(8,128)}, f32[27,128,128]{2,1,0:T(8,128)}) custom-call(f32[27,4,16,128]{3,2,1,0:T(8,128)} %pop_hbm.1, f32[27]{0:T(128)} %rates_hbm.1, s32[4,32]{1,0:T(4,128)} %bitcast.7, s32[1,128]{1,0:T(1,128)} %bitcast.8, s32[1,128]{1,0:T(1,128)} %bitcast.9, s32[1,128]{1,0:T(1,128)} %bitcast.10), custom_call_target="tpu_custom_call" | custom-call | tf_op jit(solution)/shard_map/advance/pallas_call | solution.py:458
  40.2 3.2 %arrange.1 = (f32[27,4,16,128]{3,2,1,0:T(8,128)}, f32[3456,128]{1,0:T(8,128)}) custom-call(f32[27,4,16,128]{3,2,1,0:T(8,128)} %get-tuple-element.6.adv_ref, f32[27,128,128]{2,1,0:T(8,128)} %get-tuple-element.7.got_hbm), custom_call_target="tpu_custom_call" | custom-call | tf_op jit(solution)/shard_map/arrange/pallas_call | solution.py:489

commit v8 on v7

--- a/solution.py
+++ b/solution.py
@@ -410,10 +410,10 @@
 def arrange(adv_ref, got_hbm, adv_out, ghosts_hbm, got_ref, ghosts_ref, kept_ref, keep_sem, load_sem, store_sem):
     pieces = [pl.ds(0, 6), pl.ds(6, 7), pl.ds(13, 7), pl.ds(20, 7)]
     loads = [pltpu.make_async_copy(got_hbm.at[rows], got_ref.at[rows], load_sem.at[n]) for n, rows in enumerate(pieces)]
-    for load in loads:
-        load.start()
+    for n, load in enumerate(loads):
+        load.start(priority=n % 2)
     fetch = pltpu.make_async_copy(adv_ref, kept_ref, keep_sem.at[0])
-    fetch.start()
+    fetch.start(priority=1)
 
     def put(eight, i, side, zz, slot):
         base = slot * 1728 + i * 64 + zz
@@ -426,7 +426,7 @@
     def store(n, first, length):
         rows = pl.ds(first, length)
         stores.append(pltpu.make_async_copy(ghosts_ref.at[rows], ghosts_hbm.at[rows], store_sem.at[n]))
-        stores[-1].start()
+        stores[-1].start(priority=n % 2)
 
     for load in loads:
         load.wait()

time: 43.6 us -> 43.6 us (level)
  no operation moved by 1% of the time
where the time goes in v8:
time: 43.6 us; the launch traced here: 43.4 us
  Pallas kernels  42.8 us (98%)
  between operations  0.64 us (1%)
    pallas_call x1, Pallas kernels, per_device(): pl.pallas_call(advance, out_shape=(jax.ShapeDtypeStruct((27, CX, CY, NZ),...  39.6 us
    pallas_call x1, Pallas kernels, per_device(): pl.pallas_call(arrange, out_shape=(jax.ShapeDtypeStruct((27, CX, CY, NZ),...  3.19 us

profile of v8, /device:TPU:1, one launch (start us, length us, event | category | flops | bytes accessed | tf_op | source)
XLA Modules:
  0.0 43.4 jit_solution(6373027087263108300)
XLA Ops:
  0.6 39.6 %advance.1 = (f32[27,4,16,128]{3,2,1,0:T(8,128)}, f32[27,128,128]{2,1,0:T(8,128)}) custom-call(f32[27,4,16,128]{3,2,1,0:T(8,128)} %pop_hbm.1, f32[27]{0:T(128)} %rates_hbm.1, s32[4,32]{1,0:T(4,128)} %bitcast.7, s32[1,128]{1,0:T(1,128)} %bitcast.8, s32[1,128]{1,0:T(1,128)} %bitcast.9, s32[1,128]{1,0:T(1,128)} %bitcast.10), custom_call_target="tpu_custom_call" | custom-call | tf_op jit(solution)/shard_map/advance/pallas_call | solution.py:458
  40.2 3.2 %arrange.1 = (f32[27,4,16,128]{3,2,1,0:T(8,128)}, f32[3456,128]{1,0:T(8,128)}) custom-call(f32[27,4,16,128]{3,2,1,0:T(8,128)} %get-tuple-element.6.adv_ref, f32[27,128,128]{2,1,0:T(8,128)} %get-tuple-element.7.got_hbm), custom_call_target="tpu_custom_call" | custom-call | tf_op jit(solution)/shard_map/arrange/pallas_call | solution.py:489
